TPU v7x, 256 devices: a whole 4x4x8 slice. The times are simulated.
256 devices in a mesh: ctx: 32 (over x_hi, z, core), head: 8 (over x_lo, y).
Axes of the slice: x: 4 (x_hi: 2, x_lo: 2; x = x_hi * 2 + x_lo), y: 4, z: 8, core: 2. Of those that a mesh axis runs over, the one named last changes fastest.
Arguments:
- queries_one: bfloat16 [4096, 4096], P('ctx', 'head'), may hold values from -6 to 6
- grads_one: bfloat16 [4096, 4096], P('ctx', 'head'), may hold values from -6 to 6
- queries_two: bfloat16 [4096, 4096], P('ctx', 'head'), may hold values from -6 to 6
- grads_two: bfloat16 [4096, 4096], P('ctx', 'head'), may hold values from -6 to 6
- key_rows: bfloat16 [4096, 1024], P('ctx', 'head'), may hold values from -6 to 6
- value_rows: bfloat16 [4096, 1024], P('ctx', 'head'), may hold values from -6 to 6
- shared_input: bfloat16 [4096, 8192], P('ctx'), may hold values from -6 to 6
- key_weight: bfloat16 [8192, 1024], P(None, 'head'), may hold values from -0.09375 to 0.09375
- value_weight: bfloat16 [8192, 1024], P(None, 'head'), may hold values from -0.0625 to 0.0625
- block_order: int32 [64], replicated, may hold values from 0 to 63, as said below
Outputs:
- query_grad_one: bfloat16 [4096, 4096], P('ctx', 'head')
- query_grad_two: bfloat16 [4096, 4096], P('ctx', 'head')
- input_grad: bfloat16 [4096, 8192], P('ctx', 'head')
- key_weight_grad: float32 [8192, 1024], P('ctx', 'head')
- value_weight_grad: float32 [8192, 1024], P('ctx', 'head')
Inputs may be any that keep to these rules, and one draw needn't show every extreme that they name: `block_order`: each block 0 to 63 once; slots 2c and 2c + 1 hold blocks i and 63 - i for some i.
All inputs are finite; a program needn't handle non-finite values.
Results may differ from a plain program's by a relative error of at most 0.013.
Values may be sent and summed in bfloat16 or wider, within the bound.
No kernel may reach another device: no remote copies, remote signals or barrier semaphores. Data moves between devices by JAX's collectives and lax.ppermute only.
A program may use at most 128 MiB of HBM per device.

v0:
```python
import math

import jax
import jax.numpy as jnp
from jax import lax
from jax.sharding import PartitionSpec as P

H = 32
KV = 8
DH = 128


def attend(queries, grads, query_pos, keys_pos, values_pos, key_pos, scale):
    scores = (
        jnp.einsum("rkgd,jkd->kgrj", queries, keys_pos, preferred_element_type=jnp.float32) * scale
    )
    allowed = key_pos[None, :] <= query_pos[:, None]
    scores = jnp.where(allowed, scores, -jnp.inf)
    peak = jnp.max(scores, axis=-1, keepdims=True)
    weights = jnp.exp(scores - peak)
    probabilities = weights / jnp.sum(weights, axis=-1, keepdims=True)
    prob_low = probabilities.astype(jnp.bfloat16)
    dprob = jnp.einsum("rkgd,jkd->kgrj", grads, values_pos, preferred_element_type=jnp.float32)
    row_delta = jnp.sum(probabilities * dprob, axis=-1, keepdims=True)
    dscore = (probabilities * (dprob - row_delta) * scale).astype(jnp.bfloat16)
    dquery = jnp.einsum(
        "kgrj,jkd->rkgd", dscore, keys_pos, preferred_element_type=jnp.float32
    ).astype(jnp.bfloat16)
    dkey = jnp.einsum("kgrj,rkgd->jkd", dscore, queries, preferred_element_type=jnp.float32)
    dvalue = jnp.einsum("kgrj,rkgd->jkd", prob_low, grads, preferred_element_type=jnp.float32)
    return (dquery, dkey, dvalue)


def on_device(
    queries_one,
    grads_one,
    queries_two,
    grads_two,
    key_rows,
    value_rows,
    shared_input,
    key_weight,
    value_weight,
    block_order,
):
    rows_local = queries_one.shape[0]
    half_rows = rows_local // 2
    ctx_count = lax.axis_size("ctx")
    seq_len = rows_local * ctx_count
    kv_local = key_rows.shape[1] // DH
    group = H // KV
    scale = 1.0 / math.sqrt(DH)
    gathered_keys, gathered_values = (
        lax.all_gather(key_rows, "ctx", axis=0, tiled=True),
        lax.all_gather(value_rows, "ctx", axis=0, tiled=True),
    )
    inverse = jnp.argsort(block_order)

    def to_position(slotted):
        return slotted.reshape(2 * ctx_count, half_rows, kv_local * DH)[inverse].reshape(
            seq_len, kv_local, DH
        )

    def to_slot(positioned):
        return positioned.reshape(2 * ctx_count, half_rows, kv_local * DH)[block_order].reshape(
            seq_len, kv_local * DH
        )

    keys_pos = to_position(gathered_keys)
    values_pos = to_position(gathered_values)
    key_pos = jnp.arange(seq_len, dtype=jnp.int32)
    own_blocks = lax.dynamic_slice_in_dim(block_order, 2 * lax.axis_index("ctx"), 2)
    query_pos = (
        own_blocks[:, None] * half_rows + jnp.arange(half_rows, dtype=jnp.int32)[None, :]
    ).reshape(rows_local)

    def layer_grads(queries, grads):
        query_four = queries.reshape(rows_local, kv_local, group, DH)
        grad_four = grads.reshape(rows_local, kv_local, group, DH)
        dquery, dkey, dvalue = attend(
            query_four, grad_four, query_pos, keys_pos, values_pos, key_pos, scale
        )
        return (dquery.reshape(rows_local, kv_local * group * DH), to_slot(dkey), to_slot(dvalue))

    dq_one, dk_one, dv_one = layer_grads(queries_one, grads_one)
    dq_two, dk_two, dv_two = layer_grads(queries_two, grads_two)
    key_total, value_total = (
        lax.psum_scatter(dk_one + dk_two, "ctx", scatter_dimension=0, tiled=True),
        lax.psum_scatter(dv_one + dv_two, "ctx", scatter_dimension=0, tiled=True),
    )
    key_grad = key_total.astype(jnp.bfloat16)
    value_grad = value_total.astype(jnp.bfloat16)
    contract_cols = (((1,), (1,)), ((), ()))
    input_term = lax.dot_general(
        key_grad, key_weight, contract_cols, preferred_element_type=jnp.float32
    )
    input_term = input_term + lax.dot_general(
        value_grad, value_weight, contract_cols, preferred_element_type=jnp.float32
    )
    input_grad = lax.psum_scatter(input_term, "head", scatter_dimension=1, tiled=True).astype(
        jnp.bfloat16
    )
    both_grads = jnp.concatenate([key_grad, value_grad], axis=1)
    width = key_grad.shape[1]
    contract_rows = (((0,), (0,)), ((), ()))
    weight_grad = lax.psum_scatter(
        lax.dot_general(
            shared_input, both_grads, contract_rows, preferred_element_type=jnp.float32
        ),
        "ctx",
        scatter_dimension=0,
        tiled=True,
    )
    return (dq_one, dq_two, input_grad, weight_grad[:, :width], weight_grad[:, width:])


def solution(mesh):
    return jax.shard_map(
        on_device,
        mesh=mesh,
        in_specs=(
            P("ctx", "head"),
            P("ctx", "head"),
            P("ctx", "head"),
            P("ctx", "head"),
            P("ctx", "head"),
            P("ctx", "head"),
            P("ctx", None),
            P(None, "head"),
            P(None, "head"),
            P(),
        ),
        out_specs=(
            P("ctx", "head"),
            P("ctx", "head"),
            P("ctx", "head"),
            P("ctx", "head"),
            P("ctx", "head"),
        ),
        check_vma=False,
    )
```

profile of v0, /device:TPU:24, one launch (start us, length us, event | category | flops | bytes accessed | tf_op | source)
XLA Modules:
  0.0 679.5 jit_solution(15424929762015373111)
XLA Ops:
  7.2 0.0 copy-start
  7.2 0.0 all-gather.5.cloned.1.call-start
  7.2 0.7 all-gather.5.cloned.1.call-update
  7.9 0.0 all-gather.3.cloned.1.call-start
  8.0 0.7 all-gather.3.cloned.1.call-update
  8.7 0.0 reduce-scatter.5.cloned.1.call-start
  8.7 0.7 dynamic-slice_multiply_fusion
  9.5 0.1 iota_add_fusion
  9.5 0.1 add.61
  9.6 2.7 sort.17
  12.3 0.7 compare_select_fusion
  13.0 1.1 iota_compare_fusion
  14.1 76.9 %all-gather.5.cloned.1.call-done = bf16[4096,128]{1,0:T(8,128)(2,1)} async-done(((bf16[128,128]{1,0:T(8,128)(2,1)}), bf16[4096,128]{1,0:T(8,128)(2,1)}) %all-gather.5.cloned.1.call-update) | async-done | bytes 1048592 | tf_op jit(solution)/shard_map/all_gather | solution.py:55
  91.0 2.9 gather_fusion.1
  93.9 74.3 %all-gather.3.cloned.1.call-done = bf16[4096,128]{1,0:T(8,128)(2,1)} async-done(((bf16[128,128]{1,0:T(8,128)(2,1)}), bf16[4096,128]{1,0:T(8,128)(2,1)}) %all-gather.3.cloned.1.call-update) | async-done | bytes 1048592 | tf_op jit(solution)/shard_map/all_gather | solution.py:54
  168.3 2.0 gather_fusion
  170.3 2.4 fusion.48
  172.7 0.0 copy-start.10
  172.7 1.3 fusion.47
  174.0 1.1 fusion.9
  175.1 0.0 copy-done.5
  175.2 0.0 copy-done.10
  175.2 5.1 fusion.4
  180.2 5.5 fusion.12
  185.7 0.0 copy-start.1
  185.7 0.0 copy-start.9
  185.8 2.7 fusion.29
  188.4 1.1 fusion.11
  189.6 4.3 fusion
  193.9 4.7 fusion.13
  198.6 1.9 copy-done.2
  200.5 2.6 fusion.23
  203.1 3.6 gather_fusion.2
  206.7 3.6 gather_fusion.3
  210.4 4.1 add.63
  214.5 0.0 reduce-scatter.5.cloned.1.call-update
  214.5 0.3 reduce-scatter.7.cloned.1.call-start
  214.8 6.2 fusion.14
  221.0 3.6 gather_fusion.5
  224.6 6.4 fusion.16
  231.0 3.6 gather_fusion.4
  234.6 4.1 add.65
  238.7 0.0 reduce-scatter.7.cloned.1.call-update
  238.7 0.0 reduce-scatter.9.cloned.1.call-start
  238.8 91.9 %reduce-scatter.5.cloned.1.call-done = f32[128,128]{1,0:T(8,128)} async-done(((f32[4096,128]{1,0:T(8,128)}), f32[128,128]{1,0:T(8,128)}) %reduce-scatter.5.cloned.1.call-update) | async-done | bytes 65552 | tf_op jit(solution)/shard_map/reduce_scatter | solution.py:88
  330.7 0.8 convert_element_type.47
  331.6 4.3 fusion.49
  335.8 116.7 %reduce-scatter.7.cloned.1.call-done = f32[128,128]{1,0:T(8,128)} async-done(((f32[4096,128]{1,0:T(8,128)}), f32[128,128]{1,0:T(8,128)}) %reduce-scatter.7.cloned.1.call-update) | async-done | bytes 65552 | tf_op jit(solution)/shard_map/reduce_scatter | solution.py:89
  452.6 0.8 convert_element_type.50
  453.4 5.5 convolution_add_fusion
  458.9 0.0 reduce-scatter.9.cloned.1.call-update
  459.0 0.0 reduce-scatter.11.cloned.1.call-start
  459.0 4.5 convolution_bitcast_fusion
  463.5 0.0 reduce-scatter.11.cloned.1.call-update
  463.5 2.9 convolution_convert_fusion.1
  466.5 0.8 copy.44
  467.2 3.3 convolution_convert_fusion
  470.6 0.8 copy.45
  471.3 39.1 %reduce-scatter.9.cloned.1.call-done = f32[128,1024]{1,0:T(8,128)} async-done(((f32[128,8192]{1,0:T(8,128)}), f32[128,1024]{1,0:T(8,128)}) %reduce-scatter.9.cloned.1.call-update) | async-done | bytes 524304 | tf_op jit(solution)/shard_map/reduce_scatter | solution.py:100
  510.5 1.8 convert_element_type.51
  512.2 157.9 %reduce-scatter.11.cloned.1.call-done = f32[256,256]{0,1:T(8,128)} async-done(((f32[8192,256]{0,1:T(8,128)}), f32[256,256]{0,1:T(8,128)}) %reduce-scatter.11.cloned.1.call-update) | async-done | bytes 262160 | tf_op jit(solution)/shard_map/reduce_scatter | solution.py:106
  670.2 1.0 fusion.46
  671.2 0.8 copy.47
  671.9 0.8 copy.46
  (19 shorter events, 0.1 us)
Async XLA Ops:
  7.2 451.8 %copy-start = (bf16[128,8192]{1,0:T(8,128)(2,1)S(1)}, bf16[128,8192]{1,0:T(8,128)(2,1)}, u32[]{:S(2)}) copy-start(bf16[128,8192]{1,0:T(8,128)(2,1)} %param.16) | copy-start | bytes 6291460
  7.2 165.5 %copy-start.7 = (bf16[128,512]{1,0:T(8,128)(2,1)S(1)}, bf16[128,512]{1,0:T(8,128)(2,1)}, u32[]{:S(2)}) copy-start(bf16[128,512]{1,0:T(8,128)(2,1)} %param.10) | copy-start | bytes 393220
  7.2 83.8 %all-gather.5.cloned.1.call-start = ((), (), s32[]{:S(2)}) async-start(), calls=%async_computation.5 | async-start | bytes 1081344 | tf_op jit(solution)/shard_map/all_gather | solution.py:55
  7.9 160.3 %all-gather.3.cloned.1.call-start = ((), (), s32[]{:S(2)}) async-start(), calls=%async_computation.4 | async-start | bytes 1081344 | tf_op jit(solution)/shard_map/all_gather | solution.py:54
  8.7 322.0 %reduce-scatter.5.cloned.1.call-start = ((), (), s32[]{:S(2)}) async-start(), calls=%async_computation.6 | async-start | bytes 2162688 | tf_op jit(solution)/shard_map/reduce_scatter | solution.py:88
  170.3 2.5 copy-start.6
  172.7 21.1 %copy-start.4 = (f32[1,4,128,4096]{2,3,1,0:T(8,128)}, f32[1,4,128,4096]{2,3,1,0:T(8,128)S(1)}, u32[]{:S(2)}) copy-start(f32[1,4,128,4096]{2,3,1,0:T(8,128)S(1)} %get-tuple-element.24) | copy-start | bytes 25165828
  172.7 2.4 copy-start.5
  172.7 2.4 copy-start.10
  174.0 6.2 copy-start.3
  185.7 8.1 %copy-start.1 = (bf16[4,128,4096]{1,2,0:T(8,128)(2,1)}, bf16[4,128,4096]{1,2,0:T(8,128)(2,1)S(1)}, u32[]{:S(2)}) copy-start(bf16[4,128,4096]{1,2,0:T(8,128)(2,1)S(1)} %fusion.12) | copy-start | bytes 12582916
  185.7 3.8 copy-start.9
  193.9 6.7 copy-start.8
  198.6 1.9 copy-start.2
  214.5 238.1 %reduce-scatter.7.cloned.1.call-start = ((), (), s32[]{:S(2)}) async-start(), calls=%async_computation.7 | async-start | bytes 2162688 | tf_op jit(solution)/shard_map/reduce_scatter | solution.py:89
  238.7 271.7 %reduce-scatter.9.cloned.1.call-start = ((), (), s32[]{:S(2)}) async-start(), calls=%async_computation.8 | async-start | bytes 4718592 | tf_op jit(solution)/shard_map/reduce_scatter | solution.py:100
  459.0 211.2 %reduce-scatter.11.cloned.1.call-start = ((), (), s32[]{:S(2)}) async-start(), calls=%async_computation.9 | async-start | bytes 8650752 | tf_op jit(solution)/shard_map/reduce_scatter | solution.py:106
Sparse Core Ops, SparseCore 0:
  10.8 80.1 all-gather.4
  93.8 74.4 all-gather.2
  214.6 116.0 reduce-scatter.4
  335.3 117.2 reduce-scatter.6
  459.1 51.3 reduce-scatter.8
  514.7 155.4 reduce-scatter.10
where the time goes:
time: 680 us
  waiting for transfers between devices  558 us (82%)
  matrix products  51.4 us (8%)
  other arithmetic  29.5 us (4%)
  local copies, waits for them, and re-layouts  25.4 us (4%)
  between operations  14.3 us (2%)
    reduce_scatter x1, waiting for transfers between devices, on_device(): lax.psum_scatter(lax.dot_general(shared_input, both_grads, contract_rows,...  158 us
    reduce_scatter x1, waiting for transfers between devices, on_device(): lax.psum_scatter(dv_one + dv_two, 'ctx', scatter_dimension=0, tiled=True)  117 us
    reduce_scatter x1, waiting for transfers between devices, on_device(): lax.psum_scatter(dk_one + dk_two, 'ctx', scatter_dimension=0, tiled=True)  91.9 us
    all_gather x1, waiting for transfers between devices, on_device(): lax.all_gather(value_rows, 'ctx', axis=0, tiled=True)  76.9 us
    all_gather x1, waiting for transfers between devices, on_device(): lax.all_gather(key_rows, 'ctx', axis=0, tiled=True)  74.3 us
    reduce_scatter x1, waiting for transfers between devices, on_device(): lax.psum_scatter(input_term, 'head', scatter_dimension=1, tiled=True)  39.1 us
    gather x4, local copies, waits for them, and re-layouts, to_slot(): positioned.reshape(2 * ctx_count, half_rows, kv_local * DH)[block_order]  14.5 us
  transfers between devices with their start and end apart: 6, of which 6 were waited for; matrix products, arithmetic and copies ran while one was open for 8% of the time, Pallas kernels for 0%

commit v1 on v0

v1 whole, which is shorter than its diff:
```python
import functools
import math

import jax
import jax.numpy as jnp
from jax import lax
from jax.experimental import pallas as pl
from jax.experimental.pallas import tpu as pltpu
from jax.sharding import Mesh
from jax.sharding import PartitionSpec as P

H = 32
KV = 8
DH = 128
GROUP = H // KV
CTX = ("xh", "z", "core")
CHIPS = ("xh", "z")
HEAD = ("xl", "y")
NT = (((1,), (1,)), ((), ()))
TN = (((0,), (0,)), ((), ()))
f32 = jnp.float32
bf16 = jnp.bfloat16


def attention_kernel(
    order, where, q1, g1, q2, g2, own, other, dq1, dq2, keep, send,
    kpos, vpos, weight, dprob, dk, dv, q_all, g_all, *, tile_rows,
):
    half = q1.shape[0] // 2
    chips = own.shape[0]
    n_blocks = order.shape[0]
    rows = 2 * GROUP * half
    per = tile_rows // half
    scale = 1.0 / math.sqrt(DH)
    to_log2 = scale * math.log2(math.e)
    core = where[1]

    def block(j):
        return pl.ds(pl.multiple_of(j * half, half), half)

    def tile(t):
        return pl.ds(pl.multiple_of(t * tile_rows, tile_rows), tile_rows)

    def sort(m, _):
        for ref, at in ((own, core), (other, 1 - core)):
            for i in range(2):
                to = block(order[4 * m + 2 * at + i])
                kpos[to, :] = ref[m, i * half:(i + 1) * half, :DH]
                vpos[to, :] = ref[m, i * half:(i + 1) * half, DH:]
        return 0

    lax.fori_loop(0, chips, sort, 0, unroll=2)
    first = where[0]
    upper = jnp.where(order[first] > order[first + 1], 0, 1)

    def part(at, fresh):
        p = order[first + at]
        mine = block(at)
        for i, (q_ref, g_ref) in enumerate(((q1, g1), (q2, g2))):
            for h in range(GROUP):
                r = (i * GROUP + h) * half
                q_all[r:r + half, :] = q_ref[mine, h * DH:(h + 1) * DH]
                g_all[r:r + half, :] = g_ref[mine, h * DH:(h + 1) * DH]
        last = lax.div(p, per)
        q = q_all[...]
        g = g_all[...]

        def fold(x, op):
            return op(x.reshape(tile_rows // 8, 8, rows), axis=0)

        def score(t, peak, masked):
            s = lax.dot_general(kpos[tile(t), :], q, NT, preferred_element_type=f32)
            if masked:
                key = t * tile_rows + lax.broadcasted_iota(jnp.int32, s.shape, 0)
                row = p * half + lax.rem(lax.broadcasted_iota(jnp.int32, s.shape, 1), half)
                s = jnp.where(key <= row, s, -jnp.inf)
            weight[tile(t), :] = s
            return jnp.maximum(peak, fold(s, jnp.max))

        peak = jnp.full((8, rows), -jnp.inf, f32)
        peak = lax.fori_loop(0, last, lambda t, m: score(t, m, False), peak)
        peak = score(last, peak, True)
        peak = jnp.max(peak, axis=0, keepdims=True) * to_log2

        def weigh(t, carry):
            total, delta = carry
            e = jnp.exp2(weight[tile(t), :] * to_log2 - peak)
            d = lax.dot_general(vpos[tile(t), :], g, NT, preferred_element_type=f32)
            weight[tile(t), :] = e
            dprob[tile(t), :] = d
            return total + fold(e, jnp.sum), delta + fold(e * d, jnp.sum)

        zero = jnp.zeros((8, rows), f32)
        total, delta = lax.fori_loop(0, last + 1, weigh, (zero, zero))
        share = 1.0 / jnp.sum(total, axis=0, keepdims=True)
        delta = jnp.sum(delta, axis=0, keepdims=True) * share

        def grads(t, dq):
            prob = weight[tile(t), :] * share
            ds = (prob * (dprob[tile(t), :] - delta) * scale).astype(bf16)
            dv_tile = jnp.dot(prob.astype(bf16), g, preferred_element_type=f32)
            dk_tile = jnp.dot(ds, q, preferred_element_type=f32)
            if fresh:
                dv[tile(t), :] = dv_tile
                dk[tile(t), :] = dk_tile
            else:
                dv[tile(t), :] += dv_tile
                dk[tile(t), :] += dk_tile
            return dq + lax.dot_general(kpos[tile(t), :], ds, TN, preferred_element_type=f32)

        dq = lax.fori_loop(0, last + 1, grads, jnp.zeros((DH, rows), f32))
        if fresh:

            def clear(t, _):
                dv[tile(t), :] = jnp.zeros((tile_rows, DH), f32)
                dk[tile(t), :] = jnp.zeros((tile_rows, DH), f32)
                return 0

            lax.fori_loop(last + 1, n_blocks // per, clear, 0)
        dq = dq.T.astype(bf16)
        for i, out in enumerate((dq1, dq2)):
            for h in range(GROUP):
                r = (i * GROUP + h) * half
                out[mine, h * DH:(h + 1) * DH] = dq[r:r + half, :]

    part(upper, True)
    part(1 - upper, False)

    def unsort(m, _):
        for ref, at in ((keep, core), (send, 1 - core)):
            for i in range(2):
                of = block(order[4 * m + 2 * at + i])
                ref[m, i * half:(i + 1) * half, :DH] = dk[of, :].astype(bf16)
                ref[m, i * half:(i + 1) * half, DH:] = dv[of, :].astype(bf16)
        return 0

    lax.fori_loop(0, chips, unsort, 0, unroll=2)


def attention(order, where, q1, g1, q2, g2, own, other):
    chips, rows, width = own.shape
    seq = 2 * chips * rows
    every = GROUP * rows
    vmem = pl.BlockSpec(memory_space=pltpu.VMEM)
    smem = pl.BlockSpec(memory_space=pltpu.SMEM)
    return pl.pallas_call(
        functools.partial(attention_kernel, tile_rows=512),
        out_shape=(
            jax.ShapeDtypeStruct(q1.shape, bf16),
            jax.ShapeDtypeStruct(q2.shape, bf16),
            jax.ShapeDtypeStruct(own.shape, bf16),
            jax.ShapeDtypeStruct(own.shape, bf16),
        ),
        in_specs=[smem] * 2 + [vmem] * 6,
        out_specs=(vmem,) * 4,
        scratch_shapes=[
            pltpu.VMEM((seq, DH), bf16),
            pltpu.VMEM((seq, DH), bf16),
            pltpu.VMEM((seq, every), f32),
            pltpu.VMEM((seq, every), f32),
            pltpu.VMEM((seq, DH), f32),
            pltpu.VMEM((seq, DH), f32),
            pltpu.VMEM((every, DH), bf16),
            pltpu.VMEM((every, DH), bf16),
        ],
        compiler_params=pltpu.CompilerParams(vmem_limit_bytes=48 * 2**20),
        cost_estimate=pl.CostEstimate(
            flops=10 * seq * every * DH // 2, bytes_accessed=6 * 2**20, transcendentals=seq * every // 2
        ),
    )(order, where, q1, g1, q2, g2, own, other)


def input_terms_kernel(grad, key_weight, value_weight, out):
    terms = lax.dot_general(grad[:, :DH], key_weight[...], NT, preferred_element_type=f32)
    terms += lax.dot_general(grad[:, DH:], value_weight[...], NT, preferred_element_type=f32)
    out[0] = terms.astype(bf16)


def input_terms(grad, key_weight, value_weight, parts):
    rows = grad.shape[0]
    columns = key_weight.shape[0] // parts
    return pl.pallas_call(
        input_terms_kernel,
        grid=(parts,),
        out_shape=jax.ShapeDtypeStruct((parts, rows, columns), bf16),
        in_specs=[
            pl.BlockSpec(grad.shape, lambda j: (0, 0)),
            pl.BlockSpec((columns, DH), lambda j: (j, 0)),
            pl.BlockSpec((columns, DH), lambda j: (j, 0)),
        ],
        out_specs=pl.BlockSpec((1, rows, columns), lambda j: (j, 0, 0)),
        cost_estimate=pl.CostEstimate(
            flops=4 * rows * DH * key_weight.shape[0], bytes_accessed=6 * 2**20, transcendentals=0
        ),
    )(grad, key_weight, value_weight)


def swap(x, axis):
    return lax.ppermute(x, axis, [(0, 1), (1, 0)])


def to_all(x, axes, count):
    return lax.all_to_all(jnp.broadcast_to(x[None], (count,) + x.shape), axes, 0, 0)


def on_device(
    queries_one, grads_one, queries_two, grads_two, key_rows, value_rows,
    shared_input, key_weight, value_weight, block_order,
):
    rows, width = shared_input.shape
    n_xh, n_z, n_core, n_xl, n_y = (lax.axis_size(a) for a in CTX + HEAD)
    chips, heads = n_xh * n_z, n_xl * n_y
    core, xh = lax.axis_index("core"), lax.axis_index("xh")
    head = lax.axis_index(HEAD)
    where = jnp.stack([2 * lax.axis_index(CTX), core]).astype(jnp.int32)

    with jax.named_scope("gather_keys"):
        own = to_all(jnp.concatenate([key_rows, value_rows], axis=1), CHIPS, chips)
        other = swap(own, "core")

    with jax.named_scope("spread_input"):
        piece = width // (n_xh * n_z * 4)
        cut = shared_input.reshape(rows, n_xh, n_z, 4, piece)
        cut = lax.dynamic_slice(cut, (0, head // 4, 0, head % 4, 0), (rows, 1, n_z, 1, piece))
        cut = cut.reshape(rows, n_z, piece).transpose(1, 0, 2)
        cut = lax.all_to_all(cut, "z", 0, 0)
        cut = to_all(cut.reshape(n_z * rows, piece), HEAD, heads)

    with jax.named_scope("attention"):
        dq_one, dq_two, keep, send = attention(
            block_order, where, queries_one, grads_one, queries_two, grads_two, own, other
        )
    with jax.named_scope("scatter_grads"):
        both = (keep.astype(f32) + swap(send, "core").astype(f32)).astype(bf16)
        both = lax.all_to_all(both, CHIPS, 0, 0)
        grad = jnp.sum(both.astype(f32), axis=0).astype(bf16)

    with jax.named_scope("input_grad"):
        terms = lax.all_to_all(input_terms(grad, key_weight, value_weight, heads), HEAD, 0, 0)
        input_grad = jnp.sum(terms.astype(f32), axis=0).astype(bf16)

    with jax.named_scope("weight_grad"):
        ring = to_all(grad, "z", n_z).reshape(n_z * rows, 2 * DH)
        terms = jnp.einsum("hrc,rn->hcn", cut, ring, preferred_element_type=f32)
        terms = terms.reshape(n_xh, n_core, 2 * piece, 2 * DH)
        kept = lax.dynamic_index_in_dim(terms, core, 1, keepdims=False)
        sent = lax.dynamic_index_in_dim(terms, 1 - core, 1, keepdims=False).astype(bf16)
        terms = kept + swap(sent, "core").astype(f32)
        kept = lax.dynamic_index_in_dim(terms, xh, 0, keepdims=False)
        sent = lax.dynamic_index_in_dim(terms, 1 - xh, 0, keepdims=False).astype(bf16)
        weight_grad = kept + swap(sent, "xh").astype(f32)
    return (dq_one, dq_two, input_grad, weight_grad[:, :DH], weight_grad[:, DH:])


def solution(mesh):
    fine = Mesh(mesh.devices.reshape(2, 8, 2, 2, 4), CTX + HEAD)
    both = P(CTX, HEAD)
    return jax.shard_map(
        on_device,
        mesh=fine,
        in_specs=(both,) * 6 + (P(CTX, None), P(None, HEAD), P(None, HEAD), P()),
        out_specs=(both,) * 5,
        check_vma=False,
    )
```

time: 680 us -> 206 us (0.30)
  waiting for transfers between devices: 558 us -> 96.2 us
  matrix products: 51.4 us -> 2.38 us
  blocking collectives: 0 us -> 39.3 us
  starting transfers between devices: 0.46 us -> 26.8 us
  other arithmetic: 29.5 us -> 4.48 us
  Pallas kernels: 0 us -> 20.1 us
  between operations: 14.3 us -> 0.76 us
  local copies, waits for them, and re-layouts: 25.4 us -> 14.8 us
    reduce_scatter x4 -> x0, waiting for transfers between devices: 406 us -> none  [the longest x1 158 us: on_device(): lax.psum_scatter(lax.dot_general(shared_input, both_grads, contract_rows,...]
    all_gather x2 -> x0, waiting for transfers between devices: 151 us -> none  [the longest x1 76.9 us: on_device(): lax.all_gather(value_rows, 'ctx', axis=0, tiled=True)]
    all_to_all x0 -> x5, waiting for transfers between devices: none -> 71.5 us  [the longest x2 31.5 us: to_all(): lax.all_to_all(jnp.broadcast_to(x[None], (count,) + x.shape), axes, 0, 0)]
    dot_general x13 -> x1, matrix products: 51.4 us -> 2.38 us  [on_device(): terms = jnp.einsum('hrc,rn->hcn', cut, ring, preferred_element_type=f32)]
    all_to_all x0 -> x1, blocking collectives: none -> 39.3 us  [to_all(): lax.all_to_all(jnp.broadcast_to(x[None], (count,) + x.shape), axes, 0, 0)]
    ppermute x0 -> x4, waiting for transfers between devices: none -> 24.7 us  [swap(): return lax.ppermute(x, axis, [(0, 1), (1, 0)])]
    all_to_all x0 -> x5, starting transfers between devices: none -> 23.5 us  [the longest x2 9.59 us: to_all(): lax.all_to_all(jnp.broadcast_to(x[None], (count,) + x.shape), axes, 0, 0)]
    pallas_call x0 -> x2, Pallas kernels: none -> 20.1 us  [the longest x1 13.1 us: attention(): pl.pallas_call(functools.partial(attention_kernel, tile_rows=512), out_sh...]
  transfers between devices with their start and end apart: 6 -> 9, of which waited for: 6 -> 7; matrix products, arithmetic and copies ran while one was open for 8% -> 6% of each run, Pallas kernels for 0% -> 3%
where the time goes in v1:
time: 206 us; the launch traced here: 205 us
  waiting for transfers between devices  96.2 us (47%)
  blocking collectives  39.3 us (19%)
  starting transfers between devices  26.8 us (13%)
  Pallas kernels  20.1 us (10%)
  local copies, waits for them, and re-layouts  14.8 us (7%)
  other arithmetic  4.48 us (2%)
  matrix products  2.38 us (1%)
    all_to_all x1, blocking collectives, to_all(): lax.all_to_all(jnp.broadcast_to(x[None], (count,) + x.shape), axes, 0, 0)  39.3 us
    all_to_all x2, waiting for transfers between devices, to_all(): lax.all_to_all(jnp.broadcast_to(x[None], (count,) + x.shape), axes, 0, 0)  31.5 us
    all_to_all x1, waiting for transfers between devices, on_device(): both = lax.all_to_all(both, CHIPS, 0, 0)  28.9 us
    ppermute x4, waiting for transfers between devices, swap(): return lax.ppermute(x, axis, [(0, 1), (1, 0)])  24.7 us
    pallas_call x1, Pallas kernels, attention(): pl.pallas_call(functools.partial(attention_kernel, tile_rows=512), out_sh...  13.1 us
    all_to_all x1, waiting for transfers between devices, on_device(): cut = lax.all_to_all(cut, 'z', 0, 0)  11.1 us
    all_to_all x2, starting transfers between devices, to_all(): lax.all_to_all(jnp.broadcast_to(x[None], (count,) + x.shape), axes, 0, 0)  9.59 us
    unnamed x23, local copies, waits for them, and re-layouts  8.8 us
  transfers between devices with their start and end apart: 9, of which 7 were waited for; matrix products, arithmetic and copies ran while one was open for 6% of the time, Pallas kernels for 3%

profile of v1, /device:TPU:24, one launch (start us, length us, event | category | flops | bytes accessed | tf_op | source)
XLA Modules:
  0.0 204.9 jit_solution(3952061687471865883)
XLA Ops:
  0.6 0.0 copy-start.6
  0.6 0.0 copy-start.2
  0.7 0.0 copy-start.3
  0.7 0.0 copy-start.4
  0.7 0.8 pad_maximum_fusion
  1.5 0.1 broadcast_in_dim.8
  1.6 39.3 %all_to_all.30.own = bf16[16,128,256]{2,1,0:T(8,128)(2,1)S(1)} all-to-all(bf16[16,128,256]{2,1,0:T(8,128)(2,1)S(1)} %broadcast_in_dim.8), channel_id=1, replica_groups=mesh['xh'=2,'z'=8,'core'=2,'xl'=2,'y'=4] {'xh','z'}, dimensions={0} | all-to-all | bytes 2097152 | tf_op jit(solution)/shard_map/gather_keys/all_to_all | solution.py:203
  40.9 0.0 collective-permute-start
  40.9 0.1 pad_add_fusion.where
  41.0 2.6 %collective-permute-done.other = bf16[16,128,256]{2,1,0:T(8,128)(2,1)S(1)} collective-permute-done((bf16[16,128,256]{2,1,0:T(8,128)(2,1)S(1)}, bf16[16,128,256]{2,1,0:T(8,128)(2,1)S(1)}, u32[]{:S(2)}, u32[]{:S(2)}) %collective-permute-start) | collective-permute-done | bytes 1048608 | tf_op jit(solution)/shard_map/gather_keys/ppermute | solution.py:199
  43.5 0.0 copy-start
  43.5 1.0 copy-done
  44.5 0.0 copy-done.6
  44.5 0.0 copy-done.2
  44.5 0.0 copy-done.3
  44.5 0.0 copy-done.4
  44.5 0.0 copy-start.1
  44.5 1.2 copy-done.1
  45.8 0.0 copy-start.5
  45.8 0.9 copy-done.5
  46.7 13.1 %attention.1 = (bf16[128,512]{1,0:T(8,128)(2,1)}, bf16[128,512]{1,0:T(8,128)(2,1)}, bf16[16,128,256]{2,1,0:T(8,128)(2,1)S(1)}, bf16[16,128,256]{2,1,0:T(8,128)(2,1)S(1)}) custom-call(s32[64]{0:T(128)S(1)} %copy-done.6, s32[2]{0:T(128)S(1)} %pad_add_fusion.where, bf16[128,512]{1,0:T(8,128)(2,1)S(1)} %copy-done.2, bf16[128,512]{1,0:T(8,128)(2,1)S(1)} %copy-done.3, ...), custom_call_target="tpu_custom_call" | custom-call | flops 1342177280 | bytes 6291456 | tf_op jit(solution)/shard_map/attention/pallas_call | solution.py:146
  59.7 0.2 collective-permute-start.1
  59.9 4.1 %copy.19 = bf16[128,8192]{0,1:T(8,128)(2,1)} copy(bf16[128,8192]{1,0:T(8,128)(2,1)} %param.16) | data formatting | bytes 4194304 | tf_op args[6]
  64.0 1.0 dynamic-slice_bitcast_fusion
  65.0 0.9 copy.21
  65.8 4.1 %all-to-all-start.3 = ((bf16[8,128,128]{2,1,0:T(8,128)(2,1)}), bf16[8,128,128]{2,1,0:T(8,128)(2,1)S(1)}, u32[]{:S(2)}, u32[]{:S(2)}) async-start(bf16[8,128,128]{2,1,0:T(8,128)(2,1)} %copy.21), calls=%async_computation.3 | async-start | bytes 524288 | tf_op jit(solution)/shard_map/spread_input/all_to_all | solution.py:226
  69.9 0.0 collective-permute-done.1
  69.9 1.3 add_convert_fusion
  71.2 11.1 %all-to-all-done.3 = bf16[8,128,128]{2,1,0:T(8,128)(2,1)S(1)} async-done(((bf16[8,128,128]{2,1,0:T(8,128)(2,1)}), bf16[8,128,128]{2,1,0:T(8,128)(2,1)S(1)}, u32[]{:S(2)}, u32[]{:S(2)}) %all-to-all-start.3) | async-done | bytes 262176 | tf_op jit(solution)/shard_map/spread_input/all_to_all | solution.py:226
  82.3 3.7 %all-to-all-start.1 = ((bf16[16,128,256]{2,1,0:T(8,128)(2,1)}), bf16[16,128,256]{2,1,0:T(8,128)(2,1)S(1)}, u32[]{:S(2)}, u32[]{:S(2)}) async-start(bf16[16,128,256]{2,1,0:T(8,128)(2,1)} %add_convert_fusion), calls=%async_computation.1 | async-start | bytes 2097152 | tf_op jit(solution)/shard_map/scatter_grads/all_to_all | solution.py:235
  85.9 0.1 copy.22
  86.1 28.9 %all-to-all-done.1 = bf16[16,128,256]{2,1,0:T(8,128)(2,1)S(1)} async-done(((bf16[16,128,256]{2,1,0:T(8,128)(2,1)}), bf16[16,128,256]{2,1,0:T(8,128)(2,1)S(1)}, u32[]{:S(2)}, u32[]{:S(2)}) %all-to-all-start.1) | async-done | bytes 1048608 | tf_op jit(solution)/shard_map/scatter_grads/all_to_all | solution.py:235
  114.9 1.6 broadcast_in_dim.10
  116.5 4.7 %all-to-all-start.4 = ((bf16[8,1024,128]{1,2,0:T(8,128)(2,1)}), bf16[8,1024,128]{1,2,0:T(8,128)(2,1)S(1)}, u32[]{:S(2)}, u32[]{:S(2)}) async-start(bf16[8,1024,128]{1,2,0:T(8,128)(2,1)} %broadcast_in_dim.10), calls=%async_computation.4 | async-start | bytes 4194304 | tf_op jit(solution)/shard_map/spread_input/all_to_all | solution.py:203
  121.2 0.1 reduce_sum.24.grad
  121.4 0.0 copy-start.10
  121.4 22.2 %all-to-all-done.4 = bf16[8,1024,128]{1,2,0:T(8,128)(2,1)S(1)} async-done(((bf16[8,1024,128]{1,2,0:T(8,128)(2,1)}), bf16[8,1024,128]{1,2,0:T(8,128)(2,1)S(1)}, u32[]{:S(2)}, u32[]{:S(2)}) %all-to-all-start.4) | async-done | bytes 2097184 | tf_op jit(solution)/shard_map/spread_input/all_to_all | solution.py:203
  143.6 0.0 copy-start.7
  143.6 0.9 broadcast_in_dim.22
  144.5 4.9 %all-to-all-start.5 = ((bf16[8,128,256]{2,1,0:T(8,128)(2,1)}), bf16[8,128,256]{2,1,0:T(8,128)(2,1)S(1)}, u32[]{:S(2)}, u32[]{:S(2)}) async-start(bf16[8,128,256]{2,1,0:T(8,128)(2,1)} %broadcast_in_dim.22), calls=%async_computation.5 | async-start | bytes 1048576 | tf_op jit(solution)/shard_map/weight_grad/all_to_all | solution.py:203
  149.3 0.0 copy-done.10
  149.4 7.1 %input_grad.1 = bf16[8,128,1024]{2,1,0:T(8,128)(2,1)} custom-call(bf16[128,256]{1,0:T(8,128)(2,1)} %copy-done.10, bf16[8192,128]{1,0:T(8,128)(2,1)} %key_weight.1, bf16[8192,128]{1,0:T(8,128)(2,1)} %value_weight.1), custom_call_target="tpu_custom_call" | custom-call | flops 536870912 | bytes 6291456 | tf_op jit(solution)/shard_map/input_grad/pallas_call | solution.py:182
  156.4 0.0 copy-done.7
  156.4 9.4 %all-to-all-done.5 = bf16[8,128,256]{2,1,0:T(8,128)(2,1)S(1)} async-done(((bf16[8,128,256]{2,1,0:T(8,128)(2,1)}), bf16[8,128,256]{2,1,0:T(8,128)(2,1)S(1)}, u32[]{:S(2)}, u32[]{:S(2)}) %all-to-all-start.5) | async-done | bytes 524320 | tf_op jit(solution)/shard_map/weight_grad/all_to_all | solution.py:203
  165.8 0.0 copy-start.8
  165.8 0.8 copy-done.8
  166.6 6.2 %all-to-all-start.2 = ((bf16[8,128,1024]{2,1,0:T(8,128)(2,1)}), bf16[8,128,1024]{2,1,0:T(8,128)(2,1)S(1)}, u32[]{:S(2)}, u32[]{:S(2)}) async-start(bf16[8,128,1024]{2,1,0:T(8,128)(2,1)} %input_grad.1), calls=%async_computation.2 | async-start | bytes 4194304 | tf_op jit(solution)/shard_map/input_grad/all_to_all | solution.py:239
  172.8 2.4 %fusion.3 = f32[2,2,256,256]{3,2,1,0:T(8,128)S(1)} fusion(bf16[2,2,256,1024]{3,2,1,0:T(8,128)(2,1)} %bitcast.26, bf16[1024,256,1,1]{1,0,3,2:T(8,128)(2,1)} %bitcast.28), kind=kOutput, calls=%fused_computation.11 | convolution fusion | flops 536870912 | bytes 3670016 | tf_op jit(solution)/shard_map/weight_grad/hrc,rn->hcn/dot_general | solution.py:244
  175.2 0.7 fusion
  175.9 0.0 collective-permute-start.2
  175.9 1.7 collective-permute-done.2
  177.7 0.1 bitcast_add_fusion
  177.7 0.0 copy-start.9
  177.7 0.8 copy-done.9
  178.5 3.1 %collective-permute-start.3 = (bf16[256,256]{1,0:T(8,128)(2,1)S(1)}, bf16[256,256]{1,0:T(8,128)(2,1)S(1)}, u32[]{:S(2)}, u32[]{:S(2)}) collective-permute-start(bf16[256,256]{1,0:T(8,128)(2,1)S(1)} %fusion.1), channel_id=1, source_target_pairs={{0,128},{128,0},{1,129},{129,1},{2,130},{130,2},{3,131},{131,3},{4... | collective-permute-start | bytes 393224 | tf_op jit(solution)/shard_map/weight_grad/ppermute | solution.py:199
  181.7 20.4 %collective-permute-done.3 = bf16[256,256]{1,0:T(8,128)(2,1)S(1)} collective-permute-done((bf16[256,256]{1,0:T(8,128)(2,1)S(1)}, bf16[256,256]{1,0:T(8,128)(2,1)S(1)}, u32[]{:S(2)}, u32[]{:S(2)}) %collective-permute-start.3) | collective-permute-done | bytes 131104 | tf_op jit(solution)/shard_map/weight_grad/ppermute | solution.py:199
  202.1 1.0 bitcast_add_fusion.1
  203.0 0.7 fusion.2
  203.8 0.0 all-to-all-done.2
  203.8 1.1 reduce_sum.25
  (1 shorter events, 0.0 us)
Async XLA Ops:
  0.6 43.9 %copy-start.6 = (s32[64]{0:T(128)S(1)}, s32[64]{0:T(128)}, u32[]{:S(2)}) copy-start(s32[64]{0:T(128)} %order.1) | copy-start | bytes 772
  0.6 43.9 %copy-start.2 = (bf16[128,512]{1,0:T(8,128)(2,1)S(1)}, bf16[128,512]{1,0:T(8,128)(2,1)}, u32[]{:S(2)}) copy-start(bf16[128,512]{1,0:T(8,128)(2,1)} %q1.1) | copy-start | bytes 393220
  0.7 43.9 %copy-start.3 = (bf16[128,512]{1,0:T(8,128)(2,1)S(1)}, bf16[128,512]{1,0:T(8,128)(2,1)}, u32[]{:S(2)}) copy-start(bf16[128,512]{1,0:T(8,128)(2,1)} %g1.1) | copy-start | bytes 393220
  0.7 43.9 %copy-start.4 = (bf16[128,512]{1,0:T(8,128)(2,1)S(1)}, bf16[128,512]{1,0:T(8,128)(2,1)}, u32[]{:S(2)}) copy-start(bf16[128,512]{1,0:T(8,128)(2,1)} %q2.1) | copy-start | bytes 393220
  40.9 2.7 %collective-permute-start = (bf16[16,128,256]{2,1,0:T(8,128)(2,1)S(1)}, bf16[16,128,256]{2,1,0:T(8,128)(2,1)S(1)}, u32[]{:S(2)}, u32[]{:S(2)}) collective-permute-start(bf16[16,128,256]{2,1,0:T(8,128)(2,1)S(1)} %all_to_all.30.own), channel_id=1, source_target_pairs={{0,8},{8,0},{1,9},{9,1},{2,10},{10,2},{3,11},{11,3},{4,12},{12,4},... | collective-permute-start | bytes 3145736 | tf_op jit(solution)/shard_map/gather_keys/ppermute | solution.py:199
  43.5 1.0 copy-start
  44.5 1.2 copy-start.1
  45.8 0.9 copy-start.5
  59.7 10.1 %collective-permute-start.1 = (bf16[16,128,256]{2,1,0:T(8,128)(2,1)S(1)}, bf16[16,128,256]{2,1,0:T(8,128)(2,1)S(1)}, u32[]{:S(2)}, u32[]{:S(2)}) collective-permute-start(bf16[16,128,256]{2,1,0:T(8,128)(2,1)S(1)} %get-tuple-element.12), channel_id=1, source_target_pairs={{0,8},{8,0},{1,9},{9,1},{2,10},{10,2},{3,11},{11,3},{4,12},{12,4},... | collective-permute-start | bytes 3145736 | tf_op jit(solution)/shard_map/scatter_grads/ppermute | solution.py:199
  65.8 16.5 %all-to-all-start.3 = ((bf16[8,128,128]{2,1,0:T(8,128)(2,1)}), bf16[8,128,128]{2,1,0:T(8,128)(2,1)S(1)}, u32[]{:S(2)}, u32[]{:S(2)}) async-start(bf16[8,128,128]{2,1,0:T(8,128)(2,1)} %copy.21), calls=%async_computation.3 | async-start | bytes 524288 | tf_op jit(solution)/shard_map/spread_input/all_to_all | solution.py:226
  82.3 32.7 %all-to-all-start.1 = ((bf16[16,128,256]{2,1,0:T(8,128)(2,1)}), bf16[16,128,256]{2,1,0:T(8,128)(2,1)S(1)}, u32[]{:S(2)}, u32[]{:S(2)}) async-start(bf16[16,128,256]{2,1,0:T(8,128)(2,1)} %add_convert_fusion), calls=%async_computation.1 | async-start | bytes 2097152 | tf_op jit(solution)/shard_map/scatter_grads/all_to_all | solution.py:235
  116.5 27.0 %all-to-all-start.4 = ((bf16[8,1024,128]{1,2,0:T(8,128)(2,1)}), bf16[8,1024,128]{1,2,0:T(8,128)(2,1)S(1)}, u32[]{:S(2)}, u32[]{:S(2)}) async-start(bf16[8,1024,128]{1,2,0:T(8,128)(2,1)} %broadcast_in_dim.10), calls=%async_computation.4 | async-start | bytes 4194304 | tf_op jit(solution)/shard_map/spread_input/all_to_all | solution.py:203
  121.4 28.0 %copy-start.10 = (bf16[128,256]{1,0:T(8,128)(2,1)}, bf16[128,256]{1,0:T(8,128)(2,1)S(1)}, u32[]{:S(2)}) copy-start(bf16[128,256]{1,0:T(8,128)(2,1)S(1)} %reduce_sum.24.grad) | copy-start | bytes 196612
  143.6 12.9 %copy-start.7 = (bf16[8,1024,128]{1,2,0:T(8,128)(2,1)}, bf16[8,1024,128]{1,2,0:T(8,128)(2,1)S(1)}, u32[]{:S(2)}) copy-start(bf16[8,1024,128]{1,2,0:T(8,128)(2,1)S(1)} %all-to-all-done.4) | copy-start | bytes 6291460
  144.5 21.3 %all-to-all-start.5 = ((bf16[8,128,256]{2,1,0:T(8,128)(2,1)}), bf16[8,128,256]{2,1,0:T(8,128)(2,1)S(1)}, u32[]{:S(2)}, u32[]{:S(2)}) async-start(bf16[8,128,256]{2,1,0:T(8,128)(2,1)} %broadcast_in_dim.22), calls=%async_computation.5 | async-start | bytes 1048576 | tf_op jit(solution)/shard_map/weight_grad/all_to_all | solution.py:203
  165.8 0.8 copy-start.8
  166.6 37.2 %all-to-all-start.2 = ((bf16[8,128,1024]{2,1,0:T(8,128)(2,1)}), bf16[8,128,1024]{2,1,0:T(8,128)(2,1)S(1)}, u32[]{:S(2)}, u32[]{:S(2)}) async-start(bf16[8,128,1024]{2,1,0:T(8,128)(2,1)} %input_grad.1), calls=%async_computation.2 | async-start | bytes 4194304 | tf_op jit(solution)/shard_map/input_grad/all_to_all | solution.py:239
  175.9 1.7 collective-permute-start.2
  177.7 0.8 copy-start.9
  178.5 23.5 %collective-permute-start.3 = (bf16[256,256]{1,0:T(8,128)(2,1)S(1)}, bf16[256,256]{1,0:T(8,128)(2,1)S(1)}, u32[]{:S(2)}, u32[]{:S(2)}) collective-permute-start(bf16[256,256]{1,0:T(8,128)(2,1)S(1)} %fusion.1), channel_id=1, source_target_pairs={{0,128},{128,0},{1,129},{129,1},{2,130},{130,2},{3,131},{131,3},{4... | collective-permute-start | bytes 393224 | tf_op jit(solution)/shard_map/weight_grad/ppermute | solution.py:199

commit v2 on v1

v2 whole, which is shorter than its diff:
```python
import functools
import math

import jax
import jax.numpy as jnp
from jax import lax
from jax.experimental import pallas as pl
from jax.experimental.pallas import tpu as pltpu
from jax.sharding import Mesh
from jax.sharding import PartitionSpec as P

H = 32
KV = 8
DH = 128
GROUP = H // KV
CTX = ("xh", "z", "core")
HEAD = ("xl", "y")
NT = (((1,), (1,)), ((), ()))
TN = (((0,), (0,)), ((), ()))
f32 = jnp.float32
bf16 = jnp.bfloat16
SCALE = 1.0 / math.sqrt(DH)
TO_LOG2 = SCALE * math.log2(math.e)
LOWEST = -1e30
VMEM = pl.BlockSpec(memory_space=pltpu.VMEM)
SMEM = pl.BlockSpec(memory_space=pltpu.SMEM)


class Plan:
    def __init__(self, order, where, n_keys, half):
        self.half = half
        self.n_keys = n_keys
        self.order, self.where = order, where
        self.near = []
        for b in range(n_keys):
            slot = where[4 + b]
            self.near.append(jnp.minimum(order[slot], order[slot + 1]))
        self.rank = []
        for b in range(n_keys):
            r = jnp.int32(0)
            for o in range(n_keys):
                r += jnp.where(self.near[o] < self.near[b], 1, 0)
            self.rank.append(r)

    def key_rows(self, b, i):
        pos = self.order[self.where[4 + b] + i]
        r = self.rank[b]
        at = jnp.where(pos == self.near[b], r, 2 * self.n_keys - 1 - r)
        return pl.ds(pl.multiple_of(at * self.half, self.half), self.half)

    def limits(self, a, width):
        slot = self.where[a]
        first, second = self.order[slot], self.order[slot + 1]
        mine = jnp.minimum(first, second)
        below, upto = jnp.int32(0), jnp.int32(0)
        for near in self.near:
            below += jnp.where(near < mine, 1, 0)
            upto += jnp.where(near <= mine, 1, 0)
        early, late = upto, 2 * self.n_keys - below
        inside = lax.rem(lax.broadcasted_iota(jnp.int32, (1, width), 1), self.half)
        same = upto > below

        def last(blocks):
            return jnp.where(same, (blocks - 1) * self.half + inside, blocks * self.half - 1)

        return early, late, last(early), last(late)


def load_heads(refs, q_all, g_all, order, where, half):
    for a, (ref, lead) in enumerate(refs):
        slot = where[a]
        late_at = jnp.where(order[slot] > order[slot + 1], 0, 1)
        for part, at in ((0, late_at), (1, 1 - late_at)):
            rows = pl.ds(pl.multiple_of(at * half, half), half)
            for layer in range(2):
                for h in range(GROUP):
                    r = (layer * GROUP + h) * half
                    c = (layer * 2 * GROUP + h) * DH
                    q_all[a, part, r:r + half, :] = ref[lead + (rows, slice(c, c + DH))]
                    c += GROUP * DH
                    g_all[a, part, r:r + half, :] = ref[lead + (rows, slice(c, c + DH))]


def sort_keys(plan, kv, k_sorted, v_sorted):
    for b in range(plan.n_keys):
        for i in range(2):
            to = plan.key_rows(b, i)
            rows = slice(i * plan.half, (i + 1) * plan.half)
            k_sorted[to, :] = kv[b, rows, :DH]
            v_sorted[to, :] = kv[b, rows, DH:]


def fold(x, op):
    return op(x.reshape(x.shape[0] // 8, 8, x.shape[1]), axis=0)


def tiles(seen, n_keys, half, part):
    step = n_keys * half // 2
    if part == 0:
        return (
            (0, 2 * step, None, False),
            (2 * step, step, seen > n_keys, True),
            (3 * step, step, seen > n_keys + n_keys // 2, True),
        )
    return ((0, step, seen > 0, True), (step, step, seen > n_keys // 2, True))


def under(condition, body):
    if condition is None:
        body()
    else:
        pl.when(condition)(body)


def masked_scores(k, q, start, last, masked):
    s = lax.dot_general(k, q, NT, preferred_element_type=f32)
    if masked:
        key = start + lax.broadcasted_iota(jnp.int32, s.shape, 0)
        s = jnp.where(key <= last, s, -jnp.inf)
    return s


def stats_kernel(
    order, where, own, far, side, kv, stats, k_sorted, v_sorted, q_all, g_all, scores, peak, total, delta
):
    half = own.shape[0] // 2
    n_keys = kv.shape[0]
    width = q_all.shape[2]
    plan = Plan(order, where, n_keys, half)
    sort_keys(plan, kv, k_sorted, v_sorted)
    load_heads(
        ((own, ()), (far, ()), (side, (0,)), (side, (1,))), q_all, g_all, order, where, half
    )
    for a in range(4):
        early, late, last_early, last_late = plan.limits(a, width)
        for part, seen, last in ((0, late, last_late), (1, early, last_early)):
            q, g = q_all[a, part], g_all[a, part]
            peak[...] = jnp.full(peak.shape, LOWEST, f32)
            for start, size, condition, masked in tiles(seen, n_keys, half, part):

                def score():
                    s = masked_scores(k_sorted[start:start + size, :], q, start, last, masked)
                    scores[start:start + size, :] = s
                    peak[...] = jnp.maximum(peak[...], fold(s, jnp.max))

                under(condition, score)
            top = jnp.max(peak[...], axis=0, keepdims=True) * TO_LOG2
            total[...] = jnp.zeros(total.shape, f32)
            delta[...] = jnp.zeros(delta.shape, f32)
            for start, size, condition, masked in tiles(seen, n_keys, half, part):

                def weigh():
                    e = jnp.exp2(scores[start:start + size, :] * TO_LOG2 - top)
                    d = lax.dot_general(
                        v_sorted[start:start + size, :], g, NT, preferred_element_type=f32
                    )
                    total[...] += fold(e, jnp.sum)
                    delta[...] += fold(e * d, jnp.sum)

                under(condition, weigh)
            row = 2 * a + part
            stats[0, row:row + 1, :] = top
            stats[1, row:row + 1, :] = jnp.sum(total[...], axis=0, keepdims=True)
            stats[2, row:row + 1, :] = jnp.sum(delta[...], axis=0, keepdims=True)


def grads_kernel(
    order, where, own, far, side, kv, s_own, s_far, s_side, s_both, dq_own, dq_far, dq_side, dq_both, dkv,
    k_sorted, v_sorted, q_all, g_all, dk, dv, dq,
):
    half = own.shape[0] // 2
    n_keys = kv.shape[0]
    width = q_all.shape[2]
    plan = Plan(order, where, n_keys, half)
    sort_keys(plan, kv, k_sorted, v_sorted)
    load_heads(
        ((own, ()), (far, ()), (side, (0,)), (side, (1,))), q_all, g_all, order, where, half
    )
    dk[...] = jnp.zeros(dk.shape, f32)
    dv[...] = jnp.zeros(dv.shape, f32)
    for a, dq_out in enumerate((dq_own, dq_far, dq_side, dq_both)):
        early, late, last_early, last_late = plan.limits(a, width)
        slot = where[a]
        late_at = jnp.where(order[slot] > order[slot + 1], 0, 1)
        for part, seen, last, at in ((0, late, last_late, late_at), (1, early, last_early, 1 - late_at)):
            q, g = q_all[a, part], g_all[a, part]
            held = []
            for flip, ref in ((0, s_own), (1, s_far), (2, s_side), (3, s_both)):
                r = 2 * (a ^ flip) + part
                held.append(tuple(ref[j, r:r + 1, :] for j in range(3)))
            top = functools.reduce(jnp.maximum, (t for t, _, _ in held))
            total = sum(n * jnp.exp2(t - top) for t, n, _ in held)
            delta = sum(d * jnp.exp2(t - top) for t, _, d in held) / total
            base = top + jnp.log2(total)
            dq[...] = jnp.zeros(dq.shape, f32)
            for start, size, condition, masked in tiles(seen, n_keys, half, part):

                def grads():
                    span = slice(start, start + size)
                    k = k_sorted[span, :]
                    s = masked_scores(k, q, start, last, masked)
                    p = jnp.exp2(s * TO_LOG2 - base)
                    d = lax.dot_general(v_sorted[span, :], g, NT, preferred_element_type=f32)
                    ds = (p * (d - delta)).astype(bf16)
                    dv[span, :] += jnp.dot(p.astype(bf16), g, preferred_element_type=f32)
                    dk[span, :] += jnp.dot(ds, q, preferred_element_type=f32)
                    dq[...] += lax.dot_general(k, ds, TN, preferred_element_type=f32)

                under(condition, grads)
            turned = (dq[...] * SCALE).T.astype(dq_out.dtype)
            rows = pl.ds(pl.multiple_of(at * half, half), half)
            for j in range(2 * GROUP):
                dq_out[rows, j * DH:(j + 1) * DH] = turned[j * half:(j + 1) * half, :]
    for b in range(n_keys):
        for i in range(2):
            of = plan.key_rows(b, i)
            rows = slice(i * half, (i + 1) * half)
            dkv[b, rows, :DH] = (dk[of, :] * SCALE).astype(bf16)
            dkv[b, rows, DH:] = dv[of, :].astype(bf16)


def scratch(n_keys, rows):
    width = GROUP * rows
    return [
        pltpu.VMEM((n_keys * rows, DH), bf16),
        pltpu.VMEM((n_keys * rows, DH), bf16),
        pltpu.VMEM((4, 2, width, DH), bf16),
        pltpu.VMEM((4, 2, width, DH), bf16),
    ]


def cost(n_keys, rows, products):
    pairs = 4 * GROUP * rows * n_keys * rows
    return pl.CostEstimate(
        flops=2 * products * pairs * DH, bytes_accessed=8 * 2**20, transcendentals=pairs
    )


def attention_stats(order, where, own, far, side, kv):
    n_keys, rows, _ = kv.shape
    width = GROUP * rows
    return pl.pallas_call(
        stats_kernel,
        out_shape=jax.ShapeDtypeStruct((3, 8, width), f32),
        in_specs=[SMEM] * 2 + [VMEM] * 4,
        out_specs=VMEM,
        scratch_shapes=scratch(n_keys, rows)
        + [pltpu.VMEM((n_keys * rows, width), f32)]
        + [pltpu.VMEM((8, width), f32)] * 3,
        compiler_params=pltpu.CompilerParams(vmem_limit_bytes=24 * 2**20),
        cost_estimate=cost(n_keys, rows, 2),
    )(order, where, own, far, side, kv)


def attention_grads(order, where, own, far, side, kv, stats):
    n_keys, rows, _ = kv.shape
    width = GROUP * rows
    shape = (rows, 2 * GROUP * DH)
    return pl.pallas_call(
        grads_kernel,
        out_shape=(
            jax.ShapeDtypeStruct(shape, f32),
            jax.ShapeDtypeStruct(shape, bf16),
            jax.ShapeDtypeStruct(shape, bf16),
            jax.ShapeDtypeStruct(shape, bf16),
            jax.ShapeDtypeStruct(kv.shape, bf16),
        ),
        in_specs=[SMEM] * 2 + [VMEM] * 8,
        out_specs=(VMEM,) * 5,
        scratch_shapes=scratch(n_keys, rows)
        + [pltpu.VMEM((n_keys * rows, DH), f32)] * 2
        + [pltpu.VMEM((DH, width), f32)],
        compiler_params=pltpu.CompilerParams(vmem_limit_bytes=24 * 2**20),
        cost_estimate=cost(n_keys, rows, 5),
    )(order, where, own, far, side, kv, *stats)


def cut_kernel(at, x, out):
    out[0] = x[...]


def cut_input(x, at, count, stride, width):
    rows = x.shape[0]
    return pl.pallas_call(
        cut_kernel,
        grid_spec=pltpu.PrefetchScalarGridSpec(
            num_scalar_prefetch=1,
            grid=(count,),
            in_specs=[pl.BlockSpec((rows, width), lambda j, at: (0, at[0] + j * stride))],
            out_specs=pl.BlockSpec((1, rows, width), lambda j, at: (j, 0, 0)),
        ),
        out_shape=jax.ShapeDtypeStruct((count, rows, width), x.dtype),
    )(at, x)


def input_terms_kernel(grad, key_weight, value_weight, out):
    terms = lax.dot_general(grad[:, :DH], key_weight[...], NT, preferred_element_type=f32)
    terms += lax.dot_general(grad[:, DH:], value_weight[...], NT, preferred_element_type=f32)
    out[0] = terms.astype(bf16)


def input_terms(grad, key_weight, value_weight, parts):
    rows = grad.shape[0]
    columns = key_weight.shape[0] // parts
    return pl.pallas_call(
        input_terms_kernel,
        grid=(parts,),
        out_shape=jax.ShapeDtypeStruct((parts, rows, columns), bf16),
        in_specs=[
            pl.BlockSpec(grad.shape, lambda j: (0, 0)),
            pl.BlockSpec((columns, DH), lambda j: (j, 0)),
            pl.BlockSpec((columns, DH), lambda j: (j, 0)),
        ],
        out_specs=pl.BlockSpec((1, rows, columns), lambda j: (j, 0, 0)),
        cost_estimate=pl.CostEstimate(
            flops=4 * rows * DH * key_weight.shape[0], bytes_accessed=6 * 2**20, transcendentals=0
        ),
    )(grad, key_weight, value_weight)


def swap(x, axis):
    return lax.ppermute(x, axis, [(0, 1), (1, 0)])


def cross(x):
    return lax.ppermute(x, ("xh", "core"), [(0, 3), (1, 2), (2, 1), (3, 0)])


def to_all(x, axes, count):
    return lax.all_to_all(jnp.broadcast_to(x[None], (count,) + x.shape), axes, 0, 0)


def on_device(
    queries_one, grads_one, queries_two, grads_two, key_rows, value_rows,
    shared_input, key_weight, value_weight, block_order,
):
    rows, width = shared_input.shape
    n_xh, n_z, n_core, n_xl, n_y = (lax.axis_size(a) for a in CTX + HEAD)
    heads = n_xl * n_y
    core, xh, z = lax.axis_index("core"), lax.axis_index("xh"), lax.axis_index("z")
    head = lax.axis_index(HEAD)

    def slot(h, at, c):
        return 2 * ((h * n_z + at) * n_core + c)

    where = jnp.stack(
        [slot(xh, z, core), slot(1 - xh, z, core), slot(xh, z, 1 - core), slot(1 - xh, z, 1 - core)]
        + [slot(xh, b, core) for b in range(n_z)]
    ).astype(jnp.int32)

    with jax.named_scope("gather_keys"):
        kv = to_all(jnp.concatenate([key_rows, value_rows], axis=1), "z", n_z)
    with jax.named_scope("gather_queries"):
        own = jnp.concatenate([queries_one, grads_one, queries_two, grads_two], axis=1)
        far = swap(own, "xh")
        side = swap(jnp.stack([own, far]), "core")

    with jax.named_scope("cut_input"):
        piece = DH
        per = width // (n_xh * n_z * piece)
        at = (lax.div(head, per) * (n_z * per) + lax.rem(head, per)).astype(jnp.int32)
        cut = cut_input(shared_input, at.reshape(1), n_z, per, piece)

    with jax.named_scope("attention_stats"):
        stats = attention_stats(block_order, where, own, far, side, kv)
    with jax.named_scope("share_stats"):
        stats = (stats, swap(stats, "xh"), swap(stats, "core"), cross(stats))
    with jax.named_scope("spread_input"):
        cut = lax.all_to_all(cut, "z", 0, 0)
    with jax.named_scope("attention_grads"):
        stats, cut = lax.optimization_barrier((stats, cut))
        dq_own, dq_far, dq_side, dq_both, dkv = attention_grads(
            block_order, where, own, far, side, kv, stats
        )
    with jax.named_scope("spread_input"):
        cut = lax.all_gather(cut.reshape(n_z * rows, piece), HEAD)

    with jax.named_scope("scatter_grads"):
        dkv = lax.all_to_all(dkv, "z", 0, 0)
        grad = jnp.sum(dkv.astype(f32), axis=0).astype(bf16)
    with jax.named_scope("query_grads"):
        dq = dq_own + swap(dq_far, "xh").astype(f32)
        dq = (dq + swap(dq_side, "core").astype(f32) + cross(dq_both).astype(f32)).astype(bf16)
        dq_one, dq_two = dq[:, :GROUP * DH], dq[:, GROUP * DH:]

    with jax.named_scope("input_grad"):
        terms = lax.all_to_all(input_terms(grad, key_weight, value_weight, heads), HEAD, 0, 0)
        input_grad = jnp.sum(terms.astype(f32), axis=0).astype(bf16)

    with jax.named_scope("weight_grad"):
        ring = to_all(grad, "z", n_z).reshape(n_z * rows, 2 * DH)
        terms = jnp.einsum("hrc,rn->hcn", cut, ring, preferred_element_type=f32)
        terms = terms.reshape(n_xh, n_core, 2 * piece, 2 * DH)
        kept = lax.dynamic_index_in_dim(terms, core, 1, keepdims=False)
        sent = lax.dynamic_index_in_dim(terms, 1 - core, 1, keepdims=False).astype(bf16)
        terms = kept + swap(sent, "core").astype(f32)
        kept = lax.dynamic_index_in_dim(terms, xh, 0, keepdims=False)
        sent = lax.dynamic_index_in_dim(terms, 1 - xh, 0, keepdims=False).astype(bf16)
        weight_grad = kept + swap(sent, "xh").astype(f32)
    return (dq_one, dq_two, input_grad, weight_grad[:, :DH], weight_grad[:, DH:])


def solution(mesh):
    fine = Mesh(mesh.devices.reshape(2, 8, 2, 2, 4), CTX + HEAD)
    both = P(CTX, HEAD)
    return jax.shard_map(
        on_device,
        mesh=fine,
        in_specs=(both,) * 6 + (P(CTX, None), P(None, HEAD), P(None, HEAD), P()),
        out_specs=(both,) * 5,
        check_vma=False,
    )
```

time: 206 us -> 182 us (0.88); the launches traced: 205 us -> 179 us
  waiting for transfers between devices: 96.2 us -> 50 us
  blocking collectives: 39.3 us -> 25.1 us
  between operations: 0.76 us -> 14.3 us
  Pallas kernels: 20.1 us -> 30.7 us
  starting transfers between devices: 26.8 us -> 35.8 us
    all_to_all x1 -> x0, waiting for transfers between devices: 28.9 us -> none  [on_device(): both = lax.all_to_all(both, CHIPS, 0, 0)]
    ppermute x0 -> x2, waiting for transfers between devices: none -> 19.7 us  [cross(): return lax.ppermute(x, ('xh', 'core'), [(0, 3), (1, 2), (2, 1), (3, 0)])]
    ppermute x4 -> x8, waiting for transfers between devices: 24.7 us -> 9.7 us  [swap(): return lax.ppermute(x, axis, [(0, 1), (1, 0)])]
    all_to_all x1, blocking collectives: 39.3 us -> 25.1 us  [on_device(): dkv = lax.all_to_all(dkv, 'z', 0, 0)]
    all_to_all x1, waiting for transfers between devices: 11.1 us -> 0.01 us  [on_device(): cut = lax.all_to_all(cut, 'z', 0, 0)]
    all_to_all x2, waiting for transfers between devices: 31.5 us -> 20.6 us  [to_all(): lax.all_to_all(jnp.broadcast_to(x[None], (count,) + x.shape), axes, 0, 0)]
    pallas_call x1 -> x3, Pallas kernels: 13.1 us -> 23.6 us  [the longest x1 10.4 us: attention_grads(): pl.pallas_call(grads_kernel, out_shape=(jax.ShapeDtypeStruct(shape, f32),...]
    ppermute x4 -> x8, starting transfers between devices: 3.31 us -> 12.1 us  [swap(): return lax.ppermute(x, axis, [(0, 1), (1, 0)])]
  transfers between devices with their start and end apart: 9 -> 15, of which waited for: 7 -> 7; matrix products, arithmetic and copies ran while one was open for 6% -> 7% of each run, Pallas kernels for 3% -> 17%
where the time goes in v2:
time: 182 us; the launch traced here: 179 us
  waiting for transfers between devices  50 us (27%)
  starting transfers between devices  35.8 us (20%)
  Pallas kernels  30.7 us (17%)
  blocking collectives  25.1 us (14%)
  local copies, waits for them, and re-layouts  16 us (9%)
  between operations  14.3 us (8%)
  other arithmetic  4.38 us (2%)
  matrix products  2.38 us (1%)
    all_to_all x1, blocking collectives, on_device(): dkv = lax.all_to_all(dkv, 'z', 0, 0)  25.1 us
    all_to_all x2, waiting for transfers between devices, to_all(): lax.all_to_all(jnp.broadcast_to(x[None], (count,) + x.shape), axes, 0, 0)  20.6 us
    ppermute x2, waiting for transfers between devices, cross(): return lax.ppermute(x, ('xh', 'core'), [(0, 3), (1, 2), (2, 1), (3, 0)])  19.7 us
    ppermute x8, starting transfers between devices, swap(): return lax.ppermute(x, axis, [(0, 1), (1, 0)])  12.1 us
    all_to_all x2, starting transfers between devices, to_all(): lax.all_to_all(jnp.broadcast_to(x[None], (count,) + x.shape), axes, 0, 0)  12 us
    pallas_call x1, Pallas kernels, attention_grads(): pl.pallas_call(grads_kernel, out_shape=(jax.ShapeDtypeStruct(shape, f32),...  10.4 us
    ppermute x8, waiting for transfers between devices, swap(): return lax.ppermute(x, axis, [(0, 1), (1, 0)])  9.7 us
    pallas_call x1, Pallas kernels, attention_stats(): pl.pallas_call(stats_kernel, out_shape=jax.ShapeDtypeStruct((3, 8, width)...  8.97 us
  transfers between devices with their start and end apart: 15, of which 7 were waited for; matrix products, arithmetic and copies ran while one was open for 7% of the time, Pallas kernels for 17%

profile of v2, /device:TPU:24, one launch (start us, length us, event | category | flops | bytes accessed | tf_op | source)
XLA Modules:
  0.0 178.6 jit_solution(1339716759915630896)
XLA Ops:
  7.2 0.9 constant_dynamic-update-slice_fusion.3
  8.1 0.9 constant_dynamic-update-slice_fusion.2
  9.0 0.9 constant_dynamic-update-slice_fusion.1
  9.9 0.9 constant_dynamic-update-slice_fusion.own
  10.8 3.1 %collective-permute-start = (bf16[128,2048]{1,0:T(8,128)(2,1)S(1)}, bf16[128,2048]{1,0:T(8,128)(2,1)S(1)}, u32[]{:S(2)}, u32[]{:S(2)}) collective-permute-start(bf16[128,2048]{1,0:T(8,128)(2,1)S(1)} %constant_dynamic-update-slice_fusion.own), channel_id=1, source_target_pairs={{0,128},{128,0},{1,129},{129,1},{2,130},{130,2},{3,131},{131,3},{4... | collective-permute-start | bytes 1572872 | tf_op jit(solution)/shard_map/gather_queries/ppermute | solution.py:322
  13.9 0.8 pad_maximum_fusion.1
  14.7 0.9 broadcast_in_dim.4
  15.6 8.5 %all-to-all-start = ((bf16[8,128,256]{2,1,0:T(8,128)(2,1)}), bf16[8,128,256]{2,1,0:T(8,128)(2,1)S(1)}, u32[]{:S(2)}, u32[]{:S(2)}) async-start(bf16[8,128,256]{2,1,0:T(8,128)(2,1)} %broadcast_in_dim.4), calls=%async_computation | async-start | bytes 1048576 | tf_op jit(solution)/shard_map/gather_keys/all_to_all | solution.py:330
  24.1 2.0 %collective-permute-done.far = bf16[128,2048]{1,0:T(8,128)(2,1)S(1)} collective-permute-done((bf16[128,2048]{1,0:T(8,128)(2,1)S(1)}, bf16[128,2048]{1,0:T(8,128)(2,1)S(1)}, u32[]{:S(2)}, u32[]{:S(2)}) %collective-permute-start) | collective-permute-done | bytes 524320 | tf_op jit(solution)/shard_map/gather_queries/ppermute | solution.py:322
  26.1 1.1 pad_maximum_fusion
  27.2 0.0 collective-permute-start.1
  27.2 4.3 %cut_input.1 = bf16[8,128,128]{2,1,0:T(8,128)(2,1)} custom-call(s32[1]{0:T(128)} %bitcast.14.at, bf16[128,8192]{1,0:T(8,128)(2,1)} %x.1), custom_call_target="tpu_custom_call" | custom-call | tf_op jit(solution)/shard_map/cut_input/pallas_call | solution.py:284
  31.5 9.8 %all-to-all-done.kv = bf16[8,128,256]{2,1,0:T(8,128)(2,1)S(1)} async-done(((bf16[8,128,256]{2,1,0:T(8,128)(2,1)}), bf16[8,128,256]{2,1,0:T(8,128)(2,1)S(1)}, u32[]{:S(2)}, u32[]{:S(2)}) %all-to-all-start) | async-done | bytes 524320 | tf_op jit(solution)/shard_map/gather_keys/all_to_all | solution.py:330
  41.3 3.4 %all-to-all-start.1 = ((bf16[8,128,128]{2,1,0:T(8,128)(2,1)}), bf16[8,128,128]{2,1,0:T(8,128)(2,1)S(1)}, u32[]{:S(2)}, u32[]{:S(2)}) async-start(bf16[8,128,128]{2,1,0:T(8,128)(2,1)} %cut_input.1), calls=%async_computation.1 | async-start | bytes 524288 | tf_op jit(solution)/shard_map/spread_input/all_to_all | solution.py:369
  44.7 0.0 all-gather.2.cloned.1.call-start
  44.8 0.1 stack.60.where
  44.9 0.0 collective-permute-done.1.side
  44.9 0.0 copy-done.8
  44.9 9.0 %attention_stats.1.s_own = f32[3,8,512]{2,1,0:T(8,128)S(1)} custom-call(s32[64]{0:T(128)S(1)} %copy-done.8, s32[12]{0:T(128)S(1)} %stack.60.where, bf16[128,2048]{1,0:T(8,128)(2,1)S(1)} %constant_dynamic-update-slice_fusion.own, bf16[128,2048]{1,0:T(8,128)(2,1)S(1)} %collective-permute-done.far, bf16[2,128,2048]{2,1,0:T(8,128)(2,1)S(1)} %collective-permute-done.1.side, ...), custom_call_target="tpu_custom_call" | custom-call | flops 1073741824 | bytes 8388608 | tf_op jit(solution)/shard_map/attention_stats/pallas_call | solution.py:242
  53.9 1.1 collective-permute-start.2
  54.9 0.0 collective-permute-start.3
  54.9 2.7 %collective-permute-start.4 = (f32[3,8,512]{2,1,0:T(8,128)S(1)}, f32[3,8,512]{2,1,0:T(8,128)S(1)}, u32[]{:S(2)}, u32[]{:S(2)}) collective-permute-start(f32[3,8,512]{2,1,0:T(8,128)S(1)} %attention_stats.1.s_own), channel_id=1, source_target_pairs={{0,136},{8,128},{128,8},{136,0},{1,137},{9,129},{129,9},{137,1},{2... | collective-permute-start | bytes 147464 | tf_op jit(solution)/shard_map/share_stats/ppermute | solution.py:326
  57.6 0.0 all-to-all-done.1
  57.6 2.2 %collective-permute-done.2.s_far = f32[3,8,512]{2,1,0:T(8,128)S(1)} collective-permute-done((f32[3,8,512]{2,1,0:T(8,128)S(1)}, f32[3,8,512]{2,1,0:T(8,128)S(1)}, u32[]{:S(2)}, u32[]{:S(2)}) %collective-permute-start.2) | collective-permute-done | bytes 49184 | tf_op jit(solution)/shard_map/share_stats/ppermute | solution.py:322
  59.7 0.0 collective-permute-done.3.s_side
  59.8 0.6 copy-done.4
  60.4 0.0 collective-permute-done.4.s_both
  60.4 0.6 copy-done.6
  61.0 0.0 copy-done.10
  61.0 0.0 all-gather.2.cloned.1.call-update
  61.0 0.0 copy-start.5
  61.0 0.8 copy-done.5
  61.8 0.8 copy-done.7
  62.6 10.4 %attention_grads.1 = (f32[128,1024]{1,0:T(8,128)S(1)}, bf16[128,1024]{1,0:T(8,128)(2,1)S(1)}, bf16[128,1024]{1,0:T(8,128)(2,1)S(1)}, bf16[128,1024]{1,0:T(8,128)(2,1)S(1)}, bf16[8,128,256]{2,1,0:T(8,128)(2,1)S(1)}) custom-call(s32[64]{0:T(128)S(1)} %copy-done.8, s32[12]{0:T(128)S(1)} %stack.60.where, ...), custom_call_target="tpu_custom_call" | custom-call | flops 2684354560 | bytes 8388608 | tf_op jit(solution)/shard_map/attention_grads/pallas_call | solution.py:259
  73.0 0.0 copy-start
  73.0 0.7 copy-done
  73.7 0.7 copy-done.2
  74.4 25.1 %all_to_all.25 = bf16[8,128,256]{2,1,0:T(8,128)(2,1)S(1)} all-to-all(bf16[8,128,256]{2,1,0:T(8,128)(2,1)S(1)} %get-tuple-element.23), channel_id=1, replica_groups=mesh['xh'=2,'z'=8,'core'=2,'xl'=2,'y'=4] {'z'}, dimensions={0} | all-to-all | bytes 1048576 | tf_op jit(solution)/shard_map/scatter_grads/all_to_all | solution.py:379
  99.5 0.1 reduce_sum.24.grad
  99.6 0.0 copy-start.11
  99.6 0.9 broadcast_in_dim.5
  100.4 3.5 %all-to-all-start.4 = ((bf16[8,128,256]{2,1,0:T(8,128)(2,1)}), bf16[8,128,256]{2,1,0:T(8,128)(2,1)S(1)}, u32[]{:S(2)}, u32[]{:S(2)}) async-start(bf16[8,128,256]{2,1,0:T(8,128)(2,1)} %broadcast_in_dim.5), calls=%async_computation.4 | async-start | bytes 1048576 | tf_op jit(solution)/shard_map/weight_grad/all_to_all | solution.py:330
  103.9 7.1 %input_grad.1 = bf16[8,128,1024]{2,1,0:T(8,128)(2,1)} custom-call(bf16[128,256]{1,0:T(8,128)(2,1)} %copy-done.11, bf16[8192,128]{1,0:T(8,128)(2,1)} %key_weight.1, bf16[8192,128]{1,0:T(8,128)(2,1)} %value_weight.1), custom_call_target="tpu_custom_call" | custom-call | flops 536870912 | bytes 6291456 | tf_op jit(solution)/shard_map/input_grad/pallas_call | solution.py:305
  111.0 10.8 %all-to-all-done.4 = bf16[8,128,256]{2,1,0:T(8,128)(2,1)S(1)} async-done(((bf16[8,128,256]{2,1,0:T(8,128)(2,1)}), bf16[8,128,256]{2,1,0:T(8,128)(2,1)S(1)}, u32[]{:S(2)}, u32[]{:S(2)}) %all-to-all-start.4) | async-done | bytes 524320 | tf_op jit(solution)/shard_map/weight_grad/all_to_all | solution.py:330
  121.8 0.8 copy-done.9
  122.6 5.7 %all-to-all-start.3 = ((bf16[8,128,1024]{2,1,0:T(8,128)(2,1)}), bf16[8,128,1024]{2,1,0:T(8,128)(2,1)S(1)}, u32[]{:S(2)}, u32[]{:S(2)}) async-start(bf16[8,128,1024]{2,1,0:T(8,128)(2,1)} %input_grad.1), calls=%async_computation.3 | async-start | bytes 4194304 | tf_op jit(solution)/shard_map/input_grad/all_to_all | solution.py:387
  128.3 0.0 collective-permute-start.7
  128.3 0.1 collective-permute-start.6
  128.5 3.5 %collective-permute-start.5 = (bf16[128,1024]{1,0:T(8,128)(2,1)S(1)}, bf16[128,1024]{1,0:T(8,128)(2,1)}, u32[]{:S(2)}, u32[]{:S(2)}) collective-permute-start(bf16[128,1024]{1,0:T(8,128)(2,1)S(1)} %get-tuple-element.20), channel_id=1, source_target_pairs={{0,128},{128,0},{1,129},{129,1},{2,130},{130,2},{3,131},{131,3},{4... | collective-permute-start | bytes 786440 | tf_op jit(solution)/shard_map/query_grads/ppermute | solution.py:322
  132.0 3.9 %copy.16 = bf16[8,128,1024]{2,1,0:T(8,128)(2,1)} copy(bf16[8,128,1024]{1,2,0:T(8,128)(2,1)} %bitcast.37) | data formatting | bytes 4194304 | tf_op jit(solution)/shard_map/weight_grad/hrc,rn->hcn/dot_general | solution.py:392
  135.9 2.4 %fusion.4 = f32[2,2,256,256]{3,2,1,0:T(8,128)S(1)} fusion(bf16[2,2,256,1024]{3,2,1,0:T(8,128)(2,1)} %bitcast.35, bf16[1024,256,1,1]{1,0,3,2:T(8,128)(2,1)} %bitcast.36), kind=kOutput, calls=%fused_computation.15 | convolution fusion | flops 536870912 | bytes 3670016 | tf_op jit(solution)/shard_map/weight_grad/hrc,rn->hcn/dot_general | solution.py:392
  138.3 0.1 collective-permute-start.8
  138.4 19.7 %collective-permute-done.7 = bf16[128,1024]{1,0:T(8,128)(2,1)} collective-permute-done((bf16[128,1024]{1,0:T(8,128)(2,1)S(1)}, bf16[128,1024]{1,0:T(8,128)(2,1)}, u32[]{:S(2)}, u32[]{:S(2)}) %collective-permute-start.7) | collective-permute-done | bytes 262176 | tf_op jit(solution)/shard_map/query_grads/ppermute | solution.py:326
  158.1 0.0 collective-permute-done.6
  158.1 4.4 %collective-permute-done.5 = bf16[128,1024]{1,0:T(8,128)(2,1)} collective-permute-done((bf16[128,1024]{1,0:T(8,128)(2,1)S(1)}, bf16[128,1024]{1,0:T(8,128)(2,1)}, u32[]{:S(2)}, u32[]{:S(2)}) %collective-permute-start.5) | collective-permute-done | bytes 262176 | tf_op jit(solution)/shard_map/query_grads/ppermute | solution.py:322
  162.5 1.3 add_convert_fusion
  163.8 0.0 collective-permute-done.8
  163.8 0.1 bitcast_add_fusion
  163.9 4.2 %collective-permute-start.9 = (bf16[256,256]{1,0:T(8,128)(2,1)S(1)}, bf16[256,256]{1,0:T(8,128)(2,1)S(1)}, u32[]{:S(2)}, u32[]{:S(2)}) collective-permute-start(bf16[256,256]{1,0:T(8,128)(2,1)S(1)} %fusion.1), channel_id=1, source_target_pairs={{0,128},{128,0},{1,129},{129,1},{2,130},{130,2},{3,131},{131,3},{4... | collective-permute-start | bytes 393224 | tf_op jit(solution)/shard_map/weight_grad/ppermute | solution.py:322
  168.1 0.7 fusion.3
  168.8 0.0 all-to-all-done.3
  168.8 1.1 reduce_sum.25
  169.9 1.1 collective-permute-done.9
  171.0 0.7 fusion.2
  (16 shorter events, 0.1 us)
Async XLA Ops:
  10.8 15.3 %collective-permute-start = (bf16[128,2048]{1,0:T(8,128)(2,1)S(1)}, bf16[128,2048]{1,0:T(8,128)(2,1)S(1)}, u32[]{:S(2)}, u32[]{:S(2)}) collective-permute-start(bf16[128,2048]{1,0:T(8,128)(2,1)S(1)} %constant_dynamic-update-slice_fusion.own), channel_id=1, source_target_pairs={{0,128},{128,0},{1,129},{129,1},{2,130},{130,2},{3,131},{131,3},{4... | collective-permute-start | bytes 1572872 | tf_op jit(solution)/shard_map/gather_queries/ppermute | solution.py:322
  15.6 25.7 %all-to-all-start = ((bf16[8,128,256]{2,1,0:T(8,128)(2,1)}), bf16[8,128,256]{2,1,0:T(8,128)(2,1)S(1)}, u32[]{:S(2)}, u32[]{:S(2)}) async-start(bf16[8,128,256]{2,1,0:T(8,128)(2,1)} %broadcast_in_dim.4), calls=%async_computation | async-start | bytes 1048576 | tf_op jit(solution)/shard_map/gather_keys/all_to_all | solution.py:330
  26.1 18.8 %copy-start.8 = (s32[64]{0:T(128)S(1)}, s32[64]{0:T(128)}, u32[]{:S(2)}) copy-start(s32[64]{0:T(128)} %order.3) | copy-start | bytes 772
  27.2 17.7 %collective-permute-start.1 = (bf16[2,128,2048]{2,1,0:T(8,128)(2,1)}, bf16[2,128,2048]{2,1,0:T(8,128)(2,1)S(1)}, u32[]{:S(2)}, u32[]{:S(2)}) collective-permute-start(bf16[2,128,2048]{2,1,0:T(8,128)(2,1)} %pad_maximum_fusion), channel_id=1, source_target_pairs={{0,8},{8,0},{1,9},{9,1},{2,10},{10,2},{3,11},{11,3},{4,12},{12,4},... | collective-permute-start | bytes 3145736 | tf_op jit(solution)/shard_map/gather_queries/ppermute | solution.py:322
  41.3 16.3 %all-to-all-start.1 = ((bf16[8,128,128]{2,1,0:T(8,128)(2,1)}), bf16[8,128,128]{2,1,0:T(8,128)(2,1)S(1)}, u32[]{:S(2)}, u32[]{:S(2)}) async-start(bf16[8,128,128]{2,1,0:T(8,128)(2,1)} %cut_input.1), calls=%async_computation.1 | async-start | bytes 524288 | tf_op jit(solution)/shard_map/spread_input/all_to_all | solution.py:369
  44.7 87.3 %all-gather.2.cloned.1.call-start = ((), (), s32[]{:S(2)}) async-start(), calls=%async_computation.5 | async-start | bytes 2359296 | tf_op jit(solution)/shard_map/spread_input/all_gather | solution.py:376
  53.9 5.9 %collective-permute-start.2 = (f32[3,8,512]{2,1,0:T(8,128)S(1)}, f32[3,8,512]{2,1,0:T(8,128)S(1)}, u32[]{:S(2)}, u32[]{:S(2)}) collective-permute-start(f32[3,8,512]{2,1,0:T(8,128)S(1)} %attention_stats.1.s_own), channel_id=1, source_target_pairs={{0,128},{128,0},{1,129},{129,1},{2,130},{130,2},{3,131},{131,3},{4... | collective-permute-start | bytes 147464 | tf_op jit(solution)/shard_map/share_stats/ppermute | solution.py:322
  54.9 4.8 %collective-permute-start.3 = (f32[3,8,512]{2,1,0:T(8,128)S(1)}, f32[3,8,512]{2,1,0:T(8,128)S(1)}, u32[]{:S(2)}, u32[]{:S(2)}) collective-permute-start(f32[3,8,512]{2,1,0:T(8,128)S(1)} %attention_stats.1.s_own), channel_id=1, source_target_pairs={{0,8},{8,0},{1,9},{9,1},{2,10},{10,2},{3,11},{11,3},{4,12},{12,4},... | collective-permute-start | bytes 147464 | tf_op jit(solution)/shard_map/share_stats/ppermute | solution.py:322
  54.9 5.5 %collective-permute-start.4 = (f32[3,8,512]{2,1,0:T(8,128)S(1)}, f32[3,8,512]{2,1,0:T(8,128)S(1)}, u32[]{:S(2)}, u32[]{:S(2)}) collective-permute-start(f32[3,8,512]{2,1,0:T(8,128)S(1)} %attention_stats.1.s_own), channel_id=1, source_target_pairs={{0,136},{8,128},{128,8},{136,0},{1,137},{9,129},{129,9},{137,1},{2... | collective-permute-start | bytes 147464 | tf_op jit(solution)/shard_map/share_stats/ppermute | solution.py:326
  57.6 3.4 %copy-start.10 = (bf16[8,128,128]{2,1,0:T(8,128)(2,1)}, bf16[8,128,128]{2,1,0:T(8,128)(2,1)S(1)}, u32[]{:S(2)}) copy-start(bf16[8,128,128]{2,1,0:T(8,128)(2,1)S(1)} %all-to-all-done.1) | copy-start | bytes 786436
  59.8 0.6 copy-start.4
  60.4 0.6 copy-start.6
  61.0 0.8 copy-start.5
  61.8 0.8 copy-start.7
  73.0 0.7 copy-start
  73.7 0.7 copy-start.2
  99.6 4.4 %copy-start.11 = (bf16[128,256]{1,0:T(8,128)(2,1)}, bf16[128,256]{1,0:T(8,128)(2,1)S(1)}, u32[]{:S(2)}) copy-start(bf16[128,256]{1,0:T(8,128)(2,1)S(1)} %reduce_sum.24.grad) | copy-start | bytes 196612
  100.4 21.4 %all-to-all-start.4 = ((bf16[8,128,256]{2,1,0:T(8,128)(2,1)}), bf16[8,128,256]{2,1,0:T(8,128)(2,1)S(1)}, u32[]{:S(2)}, u32[]{:S(2)}) async-start(bf16[8,128,256]{2,1,0:T(8,128)(2,1)} %broadcast_in_dim.5), calls=%async_computation.4 | async-start | bytes 1048576 | tf_op jit(solution)/shard_map/weight_grad/all_to_all | solution.py:330
  111.0 17.3 %copy-start.3 = (bf16[128,1024]{1,0:T(8,128)(2,1)S(1)}, bf16[128,1024]{1,0:T(8,128)(2,1)}, u32[]{:S(2)}) copy-start(bf16[128,1024]{1,0:T(8,128)(2,1)} %copy-done.2) | copy-start | bytes 786436
  111.0 17.3 %copy-start.1 = (bf16[128,1024]{1,0:T(8,128)(2,1)S(1)}, bf16[128,1024]{1,0:T(8,128)(2,1)}, u32[]{:S(2)}) copy-start(bf16[128,1024]{1,0:T(8,128)(2,1)} %copy-done) | copy-start | bytes 786436
  121.8 0.8 copy-start.9
  122.6 46.1 %all-to-all-start.3 = ((bf16[8,128,1024]{2,1,0:T(8,128)(2,1)}), bf16[8,128,1024]{2,1,0:T(8,128)(2,1)S(1)}, u32[]{:S(2)}, u32[]{:S(2)}) async-start(bf16[8,128,1024]{2,1,0:T(8,128)(2,1)} %input_grad.1), calls=%async_computation.3 | async-start | bytes 4194304 | tf_op jit(solution)/shard_map/input_grad/all_to_all | solution.py:387
  128.3 29.8 %collective-permute-start.7 = (bf16[128,1024]{1,0:T(8,128)(2,1)S(1)}, bf16[128,1024]{1,0:T(8,128)(2,1)}, u32[]{:S(2)}, u32[]{:S(2)}) collective-permute-start(bf16[128,1024]{1,0:T(8,128)(2,1)S(1)} %copy-done.3), channel_id=1, source_target_pairs={{0,136},{8,128},{128,8},{136,0},{1,137},{9,129},{129,9},{137,1},{2... | collective-permute-start | bytes 786440 | tf_op jit(solution)/shard_map/query_grads/ppermute | solution.py:326
  128.3 29.8 %collective-permute-start.6 = (bf16[128,1024]{1,0:T(8,128)(2,1)S(1)}, bf16[128,1024]{1,0:T(8,128)(2,1)}, u32[]{:S(2)}, u32[]{:S(2)}) collective-permute-start(bf16[128,1024]{1,0:T(8,128)(2,1)S(1)} %copy-done.1), channel_id=1, source_target_pairs={{0,8},{8,0},{1,9},{9,1},{2,10},{10,2},{3,11},{11,3},{4,12},{12,4},... | collective-permute-start | bytes 786440 | tf_op jit(solution)/shard_map/query_grads/ppermute | solution.py:322
  128.5 34.0 %collective-permute-start.5 = (bf16[128,1024]{1,0:T(8,128)(2,1)S(1)}, bf16[128,1024]{1,0:T(8,128)(2,1)}, u32[]{:S(2)}, u32[]{:S(2)}) collective-permute-start(bf16[128,1024]{1,0:T(8,128)(2,1)S(1)} %get-tuple-element.20), channel_id=1, source_target_pairs={{0,128},{128,0},{1,129},{129,1},{2,130},{130,2},{3,131},{131,3},{4... | collective-permute-start | bytes 786440 | tf_op jit(solution)/shard_map/query_grads/ppermute | solution.py:322
  138.3 25.5 %collective-permute-start.8 = (bf16[2,256,256]{2,1,0:T(8,128)(2,1)S(1)}, bf16[2,256,256]{2,1,0:T(8,128)(2,1)S(1)}, u32[]{:S(2)}, u32[]{:S(2)}) collective-permute-start(bf16[2,256,256]{2,1,0:T(8,128)(2,1)S(1)} %fusion), channel_id=1, source_target_pairs={{0,8},{8,0},{1,9},{9,1},{2,10},{10,2},{3,11},{11,3},{4,12},{12,4},... | collective-permute-start | bytes 786440 | tf_op jit(solution)/shard_map/weight_grad/ppermute | solution.py:322
  163.9 7.1 %collective-permute-start.9 = (bf16[256,256]{1,0:T(8,128)(2,1)S(1)}, bf16[256,256]{1,0:T(8,128)(2,1)S(1)}, u32[]{:S(2)}, u32[]{:S(2)}) collective-permute-start(bf16[256,256]{1,0:T(8,128)(2,1)S(1)} %fusion.1), channel_id=1, source_target_pairs={{0,128},{128,0},{1,129},{129,1},{2,130},{130,2},{3,131},{131,3},{4... | collective-permute-start | bytes 393224 | tf_op jit(solution)/shard_map/weight_grad/ppermute | solution.py:322
Sparse Core Ops, SparseCore 0:
  61.1 42.1 all-gather.1

commit v3 on v2

--- a/solution.py
+++ b/solution.py
@@ -22,8 +22,11 @@
 SCALE = 1.0 / math.sqrt(DH)
 TO_LOG2 = SCALE * math.log2(math.e)
 LOWEST = -1e30
+BIG = 59 * 2**20
+SMALL = 8 * 2**20
 VMEM = pl.BlockSpec(memory_space=pltpu.VMEM)
 SMEM = pl.BlockSpec(memory_space=pltpu.SMEM)
+ANY = pl.BlockSpec(memory_space=pl.ANY)
 
 
 class Plan:
@@ -66,19 +69,25 @@
         return early, late, last(early), last(late)
 
 
-def load_heads(refs, q_all, g_all, order, where, half):
-    for a, (ref, lead) in enumerate(refs):
-        slot = where[a]
-        late_at = jnp.where(order[slot] > order[slot + 1], 0, 1)
-        for part, at in ((0, late_at), (1, 1 - late_at)):
-            rows = pl.ds(pl.multiple_of(at * half, half), half)
-            for layer in range(2):
-                for h in range(GROUP):
-                    r = (layer * GROUP + h) * half
-                    c = (layer * 2 * GROUP + h) * DH
-                    q_all[a, part, r:r + half, :] = ref[lead + (rows, slice(c, c + DH))]
-                    c += GROUP * DH
-                    g_all[a, part, r:r + half, :] = ref[lead + (rows, slice(c, c + DH))]
+def load_heads(a, ref, q_all, g_all, order, where, half):
+    slot = where[a]
+    late_at = jnp.where(order[slot] > order[slot + 1], 0, 1)
+    for part, at in ((0, late_at), (1, 1 - late_at)):
+        rows = pl.ds(pl.multiple_of(at * half, half), half)
+        for layer in range(2):
+            for h in range(GROUP):
+                r = (layer * GROUP + h) * half
+                c = (layer * 2 * GROUP + h) * DH
+                q_all[part, r:r + half, :] = ref[rows, c:c + DH]
+                c += GROUP * DH
+                g_all[part, r:r + half, :] = ref[rows, c:c + DH]
+
+
+def fetch(pairs, sems):
+    copies = [pltpu.make_async_copy(src, dst, sems.at[i]) for i, (src, dst) in enumerate(pairs)]
+    for copy in copies:
+        copy.start()
+    return copies
 
 
 def sort_keys(plan, kv, k_sorted, v_sorted):
@@ -121,20 +130,24 @@
 
 
 def stats_kernel(
-    order, where, own, far, side, kv, stats, k_sorted, v_sorted, q_all, g_all, scores, peak, total, delta
+    order, where, own, far, side, both, kv, stats, held, kv_held, k_sorted, v_sorted, q_all, g_all, sems,
+    scores, peak, total, delta,
 ):
     half = own.shape[0] // 2
     n_keys = kv.shape[0]
-    width = q_all.shape[2]
+    width = q_all.shape[1]
+    copies = fetch(
+        [(kv, kv_held)] + [(ref, held.at[a]) for a, ref in enumerate((own, far, side, both))], sems
+    )
     plan = Plan(order, where, n_keys, half)
-    sort_keys(plan, kv, k_sorted, v_sorted)
-    load_heads(
-        ((own, ()), (far, ()), (side, (0,)), (side, (1,))), q_all, g_all, order, where, half
-    )
+    copies[0].wait()
+    sort_keys(plan, kv_held, k_sorted, v_sorted)
     for a in range(4):
+        copies[1 + a].wait()
+        load_heads(a, held.at[a], q_all, g_all, order, where, half)
         early, late, last_early, last_late = plan.limits(a, width)
         for part, seen, last in ((0, late, last_late), (1, early, last_early)):
-            q, g = q_all[a, part], g_all[a, part]
+            q, g = q_all[part], g_all[part]
             peak[...] = jnp.full(peak.shape, LOWEST, f32)
             for start, size, condition, masked in tiles(seen, n_keys, half, part):
 
@@ -165,32 +178,42 @@
 
 
 def grads_kernel(
-    order, where, own, far, side, kv, s_own, s_far, s_side, s_both, dq_own, dq_far, dq_side, dq_both, dkv,
-    k_sorted, v_sorted, q_all, g_all, dk, dv, dq,
+    order, where, own, far, side, both, kv, s_own, s_far, s_side, s_both, dq_own, dq_far, dq_side, dq_both, dkv,
+    held, kv_held, k_sorted, v_sorted, q_all, g_all, sems, s_held, out_own, out_rest, out_kv, out_sems, dk, dv, dq,
 ):
     half = own.shape[0] // 2
     n_keys = kv.shape[0]
-    width = q_all.shape[2]
+    width = q_all.shape[1]
+    copies = fetch(
+        [(kv, kv_held)]
+        + [(ref, held.at[a]) for a, ref in enumerate((own, far, side, both))]
+        + [(ref, s_held.at[a]) for a, ref in enumerate((s_own, s_far, s_side, s_both))],
+        sems,
+    )
     plan = Plan(order, where, n_keys, half)
-    sort_keys(plan, kv, k_sorted, v_sorted)
-    load_heads(
-        ((own, ()), (far, ()), (side, (0,)), (side, (1,))), q_all, g_all, order, where, half
-    )
+    copies[0].wait()
+    sort_keys(plan, kv_held, k_sorted, v_sorted)
     dk[...] = jnp.zeros(dk.shape, f32)
     dv[...] = jnp.zeros(dv.shape, f32)
-    for a, dq_out in enumerate((dq_own, dq_far, dq_side, dq_both)):
+    for copy in copies[5:]:
+        copy.wait()
+    sent = []
+    for a, out in enumerate((dq_own, dq_far, dq_side, dq_both)):
+        dq_out = out_rest.at[a - 1] if a else out_own
+        copies[1 + a].wait()
+        load_heads(a, held.at[a], q_all, g_all, order, where, half)
         early, late, last_early, last_late = plan.limits(a, width)
         slot = where[a]
         late_at = jnp.where(order[slot] > order[slot + 1], 0, 1)
         for part, seen, last, at in ((0, late, last_late, late_at), (1, early, last_early, 1 - late_at)):
-            q, g = q_all[a, part], g_all[a, part]
-            held = []
-            for flip, ref in ((0, s_own), (1, s_far), (2, s_side), (3, s_both)):
+            q, g = q_all[part], g_all[part]
+            shares = []
+            for flip in range(4):
                 r = 2 * (a ^ flip) + part
-                held.append(tuple(ref[j, r:r + 1, :] for j in range(3)))
-            top = functools.reduce(jnp.maximum, (t for t, _, _ in held))
-            total = sum(n * jnp.exp2(t - top) for t, n, _ in held)
-            delta = sum(d * jnp.exp2(t - top) for t, _, d in held) / total
+                shares.append(tuple(s_held[flip, j, r:r + 1, :] for j in range(3)))
+            top = functools.reduce(jnp.maximum, (t for t, _, _ in shares))
+            total = sum(n * jnp.exp2(t - top) for t, n, _ in shares)
+            delta = sum(d * jnp.exp2(t - top) for t, _, d in shares) / total
             base = top + jnp.log2(total)
             dq[...] = jnp.zeros(dq.shape, f32)
             for start, size, condition, masked in tiles(seen, n_keys, half, part):
@@ -211,21 +234,31 @@
             rows = pl.ds(pl.multiple_of(at * half, half), half)
             for j in range(2 * GROUP):
                 dq_out[rows, j * DH:(j + 1) * DH] = turned[j * half:(j + 1) * half, :]
+        copy = pltpu.make_async_copy(dq_out, out, out_sems.at[a])
+        copy.start()
+        sent.append(copy)
     for b in range(n_keys):
         for i in range(2):
             of = plan.key_rows(b, i)
             rows = slice(i * half, (i + 1) * half)
-            dkv[b, rows, :DH] = (dk[of, :] * SCALE).astype(bf16)
-            dkv[b, rows, DH:] = dv[of, :].astype(bf16)
-
-
-def scratch(n_keys, rows):
+            out_kv[b, rows, :DH] = (dk[of, :] * SCALE).astype(bf16)
+            out_kv[b, rows, DH:] = dv[of, :].astype(bf16)
+    copy = pltpu.make_async_copy(out_kv, dkv, out_sems.at[4])
+    copy.start()
+    for copy in sent + [copy]:
+        copy.wait()
+
+
+def scratch(n_keys, rows, copies):
     width = GROUP * rows
     return [
+        pltpu.VMEM((4, rows, 4 * GROUP * DH), bf16),
+        pltpu.VMEM((n_keys, rows, 2 * DH), bf16),
         pltpu.VMEM((n_keys * rows, DH), bf16),
         pltpu.VMEM((n_keys * rows, DH), bf16),
-        pltpu.VMEM((4, 2, width, DH), bf16),
-        pltpu.VMEM((4, 2, width, DH), bf16),
+        pltpu.VMEM((2, width, DH), bf16),
+        pltpu.VMEM((2, width, DH), bf16),
+        pltpu.SemaphoreType.DMA((copies,)),
     ]
 
 
@@ -236,23 +269,23 @@
     )
 
 
-def attention_stats(order, where, own, far, side, kv):
+def attention_stats(order, where, own, far, side, both, kv):
     n_keys, rows, _ = kv.shape
     width = GROUP * rows
     return pl.pallas_call(
         stats_kernel,
         out_shape=jax.ShapeDtypeStruct((3, 8, width), f32),
-        in_specs=[SMEM] * 2 + [VMEM] * 4,
+        in_specs=[SMEM] * 2 + [ANY] * 5,
         out_specs=VMEM,
-        scratch_shapes=scratch(n_keys, rows)
+        scratch_shapes=scratch(n_keys, rows, 5)
         + [pltpu.VMEM((n_keys * rows, width), f32)]
         + [pltpu.VMEM((8, width), f32)] * 3,
-        compiler_params=pltpu.CompilerParams(vmem_limit_bytes=24 * 2**20),
+        compiler_params=pltpu.CompilerParams(vmem_limit_bytes=BIG),
         cost_estimate=cost(n_keys, rows, 2),
-    )(order, where, own, far, side, kv)
-
-
-def attention_grads(order, where, own, far, side, kv, stats):
+    )(order, where, own, far, side, both, kv)
+
+
+def attention_grads(order, where, own, far, side, both, kv, stats):
     n_keys, rows, _ = kv.shape
     width = GROUP * rows
     shape = (rows, 2 * GROUP * DH)
@@ -265,14 +298,21 @@
             jax.ShapeDtypeStruct(shape, bf16),
             jax.ShapeDtypeStruct(kv.shape, bf16),
         ),
-        in_specs=[SMEM] * 2 + [VMEM] * 8,
-        out_specs=(VMEM,) * 5,
-        scratch_shapes=scratch(n_keys, rows)
+        in_specs=[SMEM] * 2 + [ANY] * 9,
+        out_specs=(ANY,) * 5,
+        scratch_shapes=scratch(n_keys, rows, 9)
+        + [
+            pltpu.VMEM((4, 3, 8, width), f32),
+            pltpu.VMEM(shape, f32),
+            pltpu.VMEM((3,) + shape, bf16),
+            pltpu.VMEM(kv.shape, bf16),
+            pltpu.SemaphoreType.DMA((5,)),
+        ]
         + [pltpu.VMEM((n_keys * rows, DH), f32)] * 2
         + [pltpu.VMEM((DH, width), f32)],
-        compiler_params=pltpu.CompilerParams(vmem_limit_bytes=24 * 2**20),
+        compiler_params=pltpu.CompilerParams(vmem_limit_bytes=BIG),
         cost_estimate=cost(n_keys, rows, 5),
-    )(order, where, own, far, side, kv, *stats)
+    )(order, where, own, far, side, both, kv, *stats)
 
 
 def cut_kernel(at, x, out):
@@ -294,9 +334,13 @@
 
 
 def input_terms_kernel(grad, key_weight, value_weight, out):
-    terms = lax.dot_general(grad[:, :DH], key_weight[...], NT, preferred_element_type=f32)
-    terms += lax.dot_general(grad[:, DH:], value_weight[...], NT, preferred_element_type=f32)
-    out[0] = terms.astype(bf16)
+    parts, _, columns = out.shape
+    dk, dv = grad[:, :DH], grad[:, DH:]
+    for j in range(parts):
+        span = slice(j * columns, (j + 1) * columns)
+        terms = lax.dot_general(dk, key_weight[span, :], NT, preferred_element_type=f32)
+        terms += lax.dot_general(dv, value_weight[span, :], NT, preferred_element_type=f32)
+        out[j] = terms.astype(bf16)
 
 
 def input_terms(grad, key_weight, value_weight, parts):
@@ -304,18 +348,83 @@
     columns = key_weight.shape[0] // parts
     return pl.pallas_call(
         input_terms_kernel,
-        grid=(parts,),
         out_shape=jax.ShapeDtypeStruct((parts, rows, columns), bf16),
-        in_specs=[
-            pl.BlockSpec(grad.shape, lambda j: (0, 0)),
-            pl.BlockSpec((columns, DH), lambda j: (j, 0)),
-            pl.BlockSpec((columns, DH), lambda j: (j, 0)),
-        ],
-        out_specs=pl.BlockSpec((1, rows, columns), lambda j: (j, 0, 0)),
+        in_specs=[VMEM] * 3,
+        out_specs=VMEM,
+        compiler_params=pltpu.CompilerParams(vmem_limit_bytes=12 * 2**20),
         cost_estimate=pl.CostEstimate(
             flops=4 * rows * DH * key_weight.shape[0], bytes_accessed=6 * 2**20, transcendentals=0
         ),
     )(grad, key_weight, value_weight)
+
+
+def weight_terms_kernel(at, *refs):
+    *blocks, cut, kept, sent, ring = refs
+    core, z = at[0], at[1]
+    n_z = len(blocks)
+    rows = blocks[0].shape[0]
+    for k, block in enumerate(blocks):
+        source = lax.rem(z + n_z - k, n_z)
+        ring[pl.ds(pl.multiple_of(source * rows, rows), rows), :] = block[...]
+    n_xh = kept.shape[0]
+    per = cut.shape[0] // (2 * n_xh)
+    width = cut.shape[2]
+    for out, c in ((sent, 1 - core), (kept, core)):
+        for h in range(n_xh):
+            for i in range(per):
+                x = cut[(2 * h + c) * per + i]
+                terms = lax.dot_general(ring[...], x, TN, preferred_element_type=f32)
+                out[h, :, i * width:(i + 1) * width] = terms.astype(out.dtype)
+
+
+def weight_terms(at, blocks, cut, n_xh):
+    rows, columns = blocks[0].shape
+    shape = (n_xh, columns, cut.shape[0] * cut.shape[2] // (2 * n_xh))
+    return pl.pallas_call(
+        weight_terms_kernel,
+        out_shape=(jax.ShapeDtypeStruct(shape, f32), jax.ShapeDtypeStruct(shape, bf16)),
+        in_specs=[SMEM] + [VMEM] * (len(blocks) + 1),
+        out_specs=(VMEM, VMEM),
+        scratch_shapes=[pltpu.VMEM((len(blocks) * rows, columns), bf16)],
+        compiler_params=pltpu.CompilerParams(vmem_limit_bytes=12 * 2**20),
+        cost_estimate=pl.CostEstimate(
+            flops=4 * rows * len(blocks) * columns * shape[0] * shape[2], bytes_accessed=4 * 2**20, transcendentals=0
+        ),
+    )(at, *blocks, cut)
+
+
+def half_sum_kernel(at, kept, came, mine, sent):
+    xh = at[0]
+    mine[...] = kept[xh] + came[xh].astype(f32)
+    sent[...] = (kept[1 - xh] + came[1 - xh].astype(f32)).astype(bf16)
+
+
+def half_sum(at, kept, came):
+    shape = kept.shape[1:]
+    return pl.pallas_call(
+        half_sum_kernel,
+        out_shape=(jax.ShapeDtypeStruct(shape, f32), jax.ShapeDtypeStruct(shape, bf16)),
+        in_specs=[SMEM, VMEM, VMEM],
+        out_specs=(VMEM, VMEM),
+        compiler_params=pltpu.CompilerParams(vmem_limit_bytes=SMALL),
+    )(at, kept, came)
+
+
+def last_sum_kernel(mine, came, key_out, value_out):
+    total = mine[...] + came[...].astype(f32)
+    key_out[...] = total[:DH, :].T
+    value_out[...] = total[DH:, :].T
+
+
+def last_sum(mine, came):
+    shape = jax.ShapeDtypeStruct((mine.shape[1], DH), f32)
+    return pl.pallas_call(
+        last_sum_kernel,
+        out_shape=(shape, shape),
+        in_specs=[VMEM, VMEM],
+        out_specs=(VMEM, VMEM),
+        compiler_params=pltpu.CompilerParams(vmem_limit_bytes=SMALL),
+    )(mine, came)
 
 
 def swap(x, axis):
@@ -349,11 +458,15 @@
     ).astype(jnp.int32)
 
     with jax.named_scope("gather_keys"):
-        kv = to_all(jnp.concatenate([key_rows, value_rows], axis=1), "z", n_z)
+        kv = jnp.concatenate([key_rows, value_rows], axis=1)
+        kv = jnp.broadcast_to(kv[None], (n_z,) + kv.shape)
+        kv, queries_one, shared_input = lax.optimization_barrier((kv, queries_one, shared_input))
+        kv = lax.all_to_all(kv, "z", 0, 0)
     with jax.named_scope("gather_queries"):
         own = jnp.concatenate([queries_one, grads_one, queries_two, grads_two], axis=1)
         far = swap(own, "xh")
-        side = swap(jnp.stack([own, far]), "core")
+        side = swap(own, "core")
+        both = swap(far, "core")
 
     with jax.named_scope("cut_input"):
         piece = DH
@@ -362,7 +475,7 @@
         cut = cut_input(shared_input, at.reshape(1), n_z, per, piece)
 
     with jax.named_scope("attention_stats"):
-        stats = attention_stats(block_order, where, own, far, side, kv)
+        stats = attention_stats(block_order, where, own, far, side, both, kv)
     with jax.named_scope("share_stats"):
         stats = (stats, swap(stats, "xh"), swap(stats, "core"), cross(stats))
     with jax.named_scope("spread_input"):
@@ -370,17 +483,18 @@
     with jax.named_scope("attention_grads"):
         stats, cut = lax.optimization_barrier((stats, cut))
         dq_own, dq_far, dq_side, dq_both, dkv = attention_grads(
-            block_order, where, own, far, side, kv, stats
+            block_order, where, own, far, side, both, kv, stats
         )
     with jax.named_scope("spread_input"):
         cut = lax.all_gather(cut.reshape(n_z * rows, piece), HEAD)
 
     with jax.named_scope("scatter_grads"):
         dkv = lax.all_to_all(dkv, "z", 0, 0)
+        came = (swap(dq_far, "xh"), swap(dq_side, "core"), cross(dq_both))
+        dkv, came = lax.optimization_barrier((dkv, came))
         grad = jnp.sum(dkv.astype(f32), axis=0).astype(bf16)
     with jax.named_scope("query_grads"):
-        dq = dq_own + swap(dq_far, "xh").astype(f32)
-        dq = (dq + swap(dq_side, "core").astype(f32) + cross(dq_both).astype(f32)).astype(bf16)
+        dq = (dq_own + sum(x.astype(f32) for x in came)).astype(bf16)
         dq_one, dq_two = dq[:, :GROUP * DH], dq[:, GROUP * DH:]
 
     with jax.named_scope("input_grad"):
@@ -388,16 +502,14 @@
         input_grad = jnp.sum(terms.astype(f32), axis=0).astype(bf16)
 
     with jax.named_scope("weight_grad"):
-        ring = to_all(grad, "z", n_z).reshape(n_z * rows, 2 * DH)
-        terms = jnp.einsum("hrc,rn->hcn", cut, ring, preferred_element_type=f32)
-        terms = terms.reshape(n_xh, n_core, 2 * piece, 2 * DH)
-        kept = lax.dynamic_index_in_dim(terms, core, 1, keepdims=False)
-        sent = lax.dynamic_index_in_dim(terms, 1 - core, 1, keepdims=False).astype(bf16)
-        terms = kept + swap(sent, "core").astype(f32)
-        kept = lax.dynamic_index_in_dim(terms, xh, 0, keepdims=False)
-        sent = lax.dynamic_index_in_dim(terms, 1 - xh, 0, keepdims=False).astype(bf16)
-        weight_grad = kept + swap(sent, "xh").astype(f32)
-    return (dq_one, dq_two, input_grad, weight_grad[:, :DH], weight_grad[:, DH:])
+        blocks = [grad] + [
+            lax.ppermute(grad, "z", [(i, (i + k) % n_z) for i in range(n_z)]) for k in range(1, n_z)
+        ]
+        at = jnp.stack([core, z]).astype(jnp.int32)
+        kept, sent = weight_terms(at, blocks, cut, n_xh)
+        kept, sent = half_sum(xh.astype(jnp.int32).reshape(1), kept, swap(sent, "core"))
+        key_weight_grad, value_weight_grad = last_sum(kept, swap(sent, "xh"))
+    return (dq_one, dq_two, input_grad, key_weight_grad, value_weight_grad)
 
 
 def solution(mesh):

time: 182 us -> 168 us (0.923); the launches traced: 179 us -> 167 us
  blocking collectives: 25.1 us -> 0 us
  starting transfers between devices: 35.8 us -> 55.1 us
  local copies, waits for them, and re-layouts: 16 us -> 8.52 us
  Pallas kernels: 30.7 us -> 34.9 us
  matrix products: 2.38 us -> 0 us
    all_to_all x1 -> x0, blocking collectives: 25.1 us -> none  [on_device(): dkv = lax.all_to_all(dkv, 'z', 0, 0)]
    ppermute x8 -> x9, waiting for transfers between devices: 9.7 us -> 30.5 us  [swap(): return lax.ppermute(x, axis, [(0, 1), (1, 0)])]
    all_to_all x2, waiting for transfers between devices: 20.6 us -> 0.01 us  [the longest x1 0.01 us: on_device(): kv = lax.all_to_all(kv, 'z', 0, 0)]
    ppermute x0 -> x7, starting transfers between devices: none -> 15.6 us  [on_device(): lax.ppermute(grad, 'z', [(i, (i + k) % n_z) for i in range(n_z)])]
    ppermute x2, waiting for transfers between devices: 19.7 us -> 10.8 us  [cross(): return lax.ppermute(x, ('xh', 'core'), [(0, 3), (1, 2), (2, 1), (3, 0)])]
    ppermute x0 -> x7, waiting for transfers between devices: none -> 8.68 us  [on_device(): lax.ppermute(grad, 'z', [(i, (i + k) % n_z) for i in range(n_z)])]
    dot_general x1 -> x0, local copies, waits for them, and re-layouts: 3.92 us -> none  [on_device(): terms = jnp.einsum('hrc,rn->hcn', cut, ring, preferred_element_type=f32)]
    ppermute x8 -> x9, starting transfers between devices: 12.1 us -> 8.2 us  [swap(): return lax.ppermute(x, axis, [(0, 1), (1, 0)])]
  transfers between devices with their start and end apart: 15 -> 23, of which waited for: 7 -> 11; matrix products, arithmetic and copies ran while one was open for 7% -> 3% of each run, Pallas kernels for 17% -> 20%
where the time goes in v3:
time: 168 us; the launch traced here: 167 us
  starting transfers between devices  55.1 us (33%)
  waiting for transfers between devices  50 us (30%)
  Pallas kernels  34.9 us (21%)
  between operations  14.3 us (9%)
  local copies, waits for them, and re-layouts  8.52 us (5%)
  other arithmetic  3.85 us (2%)
    ppermute x9, waiting for transfers between devices, swap(): return lax.ppermute(x, axis, [(0, 1), (1, 0)])  30.5 us
    ppermute x7, starting transfers between devices, on_device(): lax.ppermute(grad, 'z', [(i, (i + k) % n_z) for i in range(n_z)])  15.6 us
    pallas_call x1, Pallas kernels, attention_grads(): pl.pallas_call(grads_kernel, out_shape=(jax.ShapeDtypeStruct(shape, f32),...  13.9 us
    pallas_call x1, Pallas kernels, attention_stats(): pl.pallas_call(stats_kernel, out_shape=jax.ShapeDtypeStruct((3, 8, width)...  11.3 us
    ppermute x2, waiting for transfers between devices, cross(): return lax.ppermute(x, ('xh', 'core'), [(0, 3), (1, 2), (2, 1), (3, 0)])  10.8 us
    ppermute x7, waiting for transfers between devices, on_device(): lax.ppermute(grad, 'z', [(i, (i + k) % n_z) for i in range(n_z)])  8.68 us
    all_to_all x1, starting transfers between devices, on_device(): kv = lax.all_to_all(kv, 'z', 0, 0)  8.47 us
    ppermute x9, starting transfers between devices, swap(): return lax.ppermute(x, axis, [(0, 1), (1, 0)])  8.2 us
  transfers between devices with their start and end apart: 23, of which 11 were waited for; matrix products, arithmetic and copies ran while one was open for 3% of the time, Pallas kernels for 20%

profile of v3, /device:TPU:24, one launch (start us, length us, event | category | flops | bytes accessed | tf_op | source)
XLA Modules:
  0.0 166.6 jit_solution(1509561684006378290)
XLA Ops:
  7.2 0.8 pad_maximum_fusion
  8.0 0.8 broadcast_in_dim.2
  8.9 8.5 %all-to-all-start = ((bf16[8,128,256]{2,1,0:T(8,128)(2,1)}), bf16[8,128,256]{2,1,0:T(8,128)(2,1)S(1)}, u32[]{:S(2)}, u32[]{:S(2)}) async-start(bf16[8,128,256]{2,1,0:T(8,128)(2,1)} %broadcast_in_dim.2), calls=%async_computation | async-start | bytes 1048576 | tf_op jit(solution)/shard_map/gather_keys/all_to_all | solution.py:464
  17.3 0.9 constant_dynamic-update-slice_fusion.3
  18.3 3.1 %collective-permute-start = (bf16[128,2048]{1,0:T(8,128)(2,1)S(1)}, bf16[128,2048]{1,0:T(8,128)(2,1)S(1)}, u32[]{:S(2)}, u32[]{:S(2)}) collective-permute-start(bf16[128,2048]{1,0:T(8,128)(2,1)S(1)} %constant_dynamic-update-slice_fusion.own), channel_id=1, source_target_pairs={{0,128},{128,0},{1,129},{129,1},{2,130},{130,2},{3,131},{131,3},{4... | collective-permute-start | bytes 1572872 | tf_op jit(solution)/shard_map/gather_queries/ppermute | solution.py:431
  21.5 0.0 collective-permute-start.1
  21.5 11.9 %collective-permute-done.far = bf16[128,2048]{1,0:T(8,128)(2,1)S(1)} collective-permute-done((bf16[128,2048]{1,0:T(8,128)(2,1)S(1)}, bf16[128,2048]{1,0:T(8,128)(2,1)S(1)}, u32[]{:S(2)}, u32[]{:S(2)}) %collective-permute-start) | collective-permute-done | bytes 524320 | tf_op jit(solution)/shard_map/gather_queries/ppermute | solution.py:431
  33.3 0.0 collective-permute-start.2
  33.3 4.4 %cut_input.1 = bf16[8,128,128]{2,1,0:T(8,128)(2,1)} custom-call(s32[1]{0:T(128)} %bitcast.12.at, bf16[128,8192]{1,0:T(8,128)(2,1)} %x), custom_call_target="tpu_custom_call" | custom-call | tf_op jit(solution)/shard_map/cut_input/pallas_call | solution.py:324
  37.7 0.0 all-to-all-done.kv
  37.7 6.9 %all-to-all-start.1 = ((bf16[8,128,128]{2,1,0:T(8,128)(2,1)}), bf16[8,128,128]{2,1,0:T(8,128)(2,1)S(1)}, u32[]{:S(2)}, u32[]{:S(2)}) async-start(bf16[8,128,128]{2,1,0:T(8,128)(2,1)} %cut_input.1), calls=%async_computation.1 | async-start | bytes 524288 | tf_op jit(solution)/shard_map/spread_input/all_to_all | solution.py:482
  44.6 0.0 all-gather.2.cloned.1.call-start
  44.7 0.7 stack.60.where
  45.4 0.0 collective-permute-done.1.side
  45.4 0.0 collective-permute-done.2.both
  45.4 0.8 copy-done.11
  46.2 0.8 copy-done.12
  47.0 11.3 %attention_stats.1.s_own = f32[3,8,512]{2,1,0:T(8,128)} custom-call(s32[64]{0:T(128)} %order.3, s32[12]{0:T(128)} %stack.60.where, bf16[128,2048]{1,0:T(8,128)(2,1)} %copy-done.9, bf16[128,2048]{1,0:T(8,128)(2,1)} %copy-done.10, bf16[128,2048]{1,0:T(8,128)(2,1)} %copy-done.11, bf16[128,2048]{1,0:T(8,128)(2,1)} %copy-done.12, bf16[8,128,256]{2,1,0:T(8,128)(2,1)} %copy-done.5), custom_call_target="tpu_custom_call" | custom-call | flops 1073741824 | bytes 8388608 | tf_op jit(solution)/shard_map/attention_stats/pallas_call | solution.py:275
  58.2 1.9 %collective-permute-start.5 = (f32[3,8,512]{2,1,0:T(8,128)}, f32[3,8,512]{2,1,0:T(8,128)S(1)}, u32[]{:S(2)}, u32[]{:S(2)}) collective-permute-start(f32[3,8,512]{2,1,0:T(8,128)} %attention_stats.1.s_own), channel_id=1, source_target_pairs={{0,136},{8,128},{128,8},{136,0},{1,137},{9,129},{129,9},{137,1},{2... | collective-permute-start | bytes 147464 | tf_op jit(solution)/shard_map/share_stats/ppermute | solution.py:435
  60.2 0.0 collective-permute-start.4
  60.2 1.8 %collective-permute-start.3 = (f32[3,8,512]{2,1,0:T(8,128)}, f32[3,8,512]{2,1,0:T(8,128)S(1)}, u32[]{:S(2)}, u32[]{:S(2)}) collective-permute-start(f32[3,8,512]{2,1,0:T(8,128)} %attention_stats.1.s_own), channel_id=1, source_target_pairs={{0,128},{128,0},{1,129},{129,1},{2,130},{130,2},{3,131},{131,3},{4... | collective-permute-start | bytes 147464 | tf_op jit(solution)/shard_map/share_stats/ppermute | solution.py:431
  62.0 0.0 all-to-all-done.1
  62.0 2.0 %collective-permute-done.5.s_both = f32[3,8,512]{2,1,0:T(8,128)S(1)} collective-permute-done((f32[3,8,512]{2,1,0:T(8,128)}, f32[3,8,512]{2,1,0:T(8,128)S(1)}, u32[]{:S(2)}, u32[]{:S(2)}) %collective-permute-start.5) | collective-permute-done | bytes 49184 | tf_op jit(solution)/shard_map/share_stats/ppermute | solution.py:435
  64.0 2.1 %collective-permute-done.3.s_far = f32[3,8,512]{2,1,0:T(8,128)S(1)} collective-permute-done((f32[3,8,512]{2,1,0:T(8,128)}, f32[3,8,512]{2,1,0:T(8,128)S(1)}, u32[]{:S(2)}, u32[]{:S(2)}) %collective-permute-start.3) | collective-permute-done | bytes 49184 | tf_op jit(solution)/shard_map/share_stats/ppermute | solution.py:431
  66.1 0.0 all-gather.2.cloned.1.call-update
  66.1 0.6 copy-done.15
  66.7 13.9 %attention_grads.1 = (f32[128,1024]{1,0:T(8,128)}, bf16[128,1024]{1,0:T(8,128)(2,1)}, bf16[128,1024]{1,0:T(8,128)(2,1)}, bf16[128,1024]{1,0:T(8,128)(2,1)}, bf16[8,128,256]{2,1,0:T(8,128)(2,1)}) custom-call(s32[64]{0:T(128)} %order.3, s32[12]{0:T(128)} %stack.60.where, bf16[128,2048]{1,0:T(8,128)(2,1)} %copy-done.9, bf16[128,2048]{1,0:T(8,128)(2,1)} %copy-done.10, ...), custom_call_target="tpu_custom_call" | custom-call | flops 2684354560 | bytes 8388608 | tf_op jit(solution)/shard_map/attention_grads/pallas_call | solution.py:292
  80.6 7.4 %all-to-all-start.2 = ((bf16[8,128,256]{2,1,0:T(8,128)(2,1)}), bf16[8,128,256]{2,1,0:T(8,128)(2,1)S(1)}, u32[]{:S(2)}, u32[]{:S(2)}) async-start(bf16[8,128,256]{2,1,0:T(8,128)(2,1)} %get-tuple-element.36), calls=%async_computation.2 | async-start | bytes 1048576 | tf_op jit(solution)/shard_map/scatter_grads/all_to_all | solution.py:492
  87.9 1.9 %collective-permute-start.6 = (bf16[128,1024]{1,0:T(8,128)(2,1)}, bf16[128,1024]{1,0:T(8,128)(2,1)S(1)}, u32[]{:S(2)}, u32[]{:S(2)}) collective-permute-start(bf16[128,1024]{1,0:T(8,128)(2,1)} %get-tuple-element.37), channel_id=1, source_target_pairs={{0,128},{128,0},{1,129},{129,1},{2,130},{130,2},{3,131},{131,3},{4... | collective-permute-start | bytes 786440 | tf_op jit(solution)/shard_map/scatter_grads/ppermute | solution.py:431
  89.8 0.0 collective-permute-start.7
  89.8 1.8 %collective-permute-start.8 = (bf16[128,1024]{1,0:T(8,128)(2,1)}, bf16[128,1024]{1,0:T(8,128)(2,1)S(1)}, u32[]{:S(2)}, u32[]{:S(2)}) collective-permute-start(bf16[128,1024]{1,0:T(8,128)(2,1)} %get-tuple-element.39), channel_id=1, source_target_pairs={{0,136},{8,128},{128,8},{136,0},{1,137},{9,129},{129,9},{137,1},{2... | collective-permute-start | bytes 786440 | tf_op jit(solution)/shard_map/scatter_grads/ppermute | solution.py:435
  91.6 12.8 %collective-permute-done.6 = bf16[128,1024]{1,0:T(8,128)(2,1)S(1)} collective-permute-done((bf16[128,1024]{1,0:T(8,128)(2,1)}, bf16[128,1024]{1,0:T(8,128)(2,1)S(1)}, u32[]{:S(2)}, u32[]{:S(2)}) %collective-permute-start.6) | collective-permute-done | bytes 262176 | tf_op jit(solution)/shard_map/scatter_grads/ppermute | solution.py:431
  104.4 0.0 collective-permute-done.7
  104.4 8.8 %collective-permute-done.8 = bf16[128,1024]{1,0:T(8,128)(2,1)S(1)} collective-permute-done((bf16[128,1024]{1,0:T(8,128)(2,1)}, bf16[128,1024]{1,0:T(8,128)(2,1)S(1)}, u32[]{:S(2)}, u32[]{:S(2)}) %collective-permute-start.8) | collective-permute-done | bytes 262176 | tf_op jit(solution)/shard_map/scatter_grads/ppermute | solution.py:435
  113.3 0.1 reduce_sum.24.grad.refs_0_
  113.3 0.0 copy-start.1
  113.4 1.6 copy-done.1
  114.9 2.6 %input_grad.1 = bf16[8,128,1024]{2,1,0:T(8,128)(2,1)} custom-call(bf16[128,256]{1,0:T(8,128)(2,1)S(1)} %reduce_sum.24.grad.refs_0_, bf16[8192,128]{1,0:T(8,128)(2,1)S(1)} %copy-done, bf16[8192,128]{1,0:T(8,128)(2,1)S(1)} %copy-done.1), custom_call_target="tpu_custom_call" | custom-call | flops 536870912 | bytes 6291456 | tf_op jit(solution)/shard_map/input_grad/pallas_call | solution.py:349
  117.6 4.7 %all-to-all-start.3 = ((bf16[8,128,1024]{2,1,0:T(8,128)(2,1)}), bf16[8,128,1024]{2,1,0:T(8,128)(2,1)}, u32[]{:S(2)}, u32[]{:S(2)}) async-start(bf16[8,128,1024]{2,1,0:T(8,128)(2,1)} %input_grad.1), calls=%async_computation.3 | async-start | bytes 4194304 | tf_op jit(solution)/shard_map/input_grad/all_to_all | solution.py:501
  122.3 3.1 %collective-permute-start.15 = (bf16[128,256]{1,0:T(8,128)(2,1)S(1)}, bf16[128,256]{1,0:T(8,128)(2,1)S(1)}, u32[]{:S(2)}, u32[]{:S(2)}) collective-permute-start(bf16[128,256]{1,0:T(8,128)(2,1)S(1)} %reduce_sum.24.grad.refs_0_), channel_id=1, source_target_pairs={{0,112},{16,0},{32,16},{48,32},{64,48},{80,64},{96,80},{112,96},{1... | collective-permute-start | bytes 196616 | tf_op jit(solution)/shard_map/weight_grad/ppermute | solution.py:506
  125.4 2.4 %collective-permute-start.14 = (bf16[128,256]{1,0:T(8,128)(2,1)S(1)}, bf16[128,256]{1,0:T(8,128)(2,1)S(1)}, u32[]{:S(2)}, u32[]{:S(2)}) collective-permute-start(bf16[128,256]{1,0:T(8,128)(2,1)S(1)} %reduce_sum.24.grad.refs_0_), channel_id=1, source_target_pairs={{0,96},{16,112},{32,0},{48,16},{64,32},{80,48},{96,64},{112,80},{1... | collective-permute-start | bytes 196616 | tf_op jit(solution)/shard_map/weight_grad/ppermute | solution.py:506
  127.8 1.1 collective-permute-start.13
  128.9 4.0 %collective-permute-start.12 = (bf16[128,256]{1,0:T(8,128)(2,1)S(1)}, bf16[128,256]{1,0:T(8,128)(2,1)S(1)}, u32[]{:S(2)}, u32[]{:S(2)}) collective-permute-start(bf16[128,256]{1,0:T(8,128)(2,1)S(1)} %reduce_sum.24.grad.refs_0_), channel_id=1, source_target_pairs={{0,64},{16,80},{32,96},{48,112},{64,0},{80,16},{96,32},{112,48},{1... | collective-permute-start | bytes 196616 | tf_op jit(solution)/shard_map/weight_grad/ppermute | solution.py:506
  132.9 0.0 collective-permute-start.11
  132.9 0.0 collective-permute-done.15.refs_7_
  132.9 3.4 %collective-permute-start.10 = (bf16[128,256]{1,0:T(8,128)(2,1)S(1)}, bf16[128,256]{1,0:T(8,128)(2,1)S(1)}, u32[]{:S(2)}, u32[]{:S(2)}) collective-permute-start(bf16[128,256]{1,0:T(8,128)(2,1)S(1)} %reduce_sum.24.grad.refs_0_), channel_id=1, source_target_pairs={{0,32},{16,48},{32,64},{48,80},{64,96},{80,112},{96,0},{112,16},{1... | collective-permute-start | bytes 196616 | tf_op jit(solution)/shard_map/weight_grad/ppermute | solution.py:506
  136.4 1.6 collective-permute-start.9
  137.9 0.1 pad_add_fusion.at
  138.0 0.0 collective-permute-done.13.refs_5_
  138.0 0.8 collective-permute-done.12.refs_4_
  138.9 4.2 %collective-permute-done.11.refs_3_ = bf16[128,256]{1,0:T(8,128)(2,1)S(1)} collective-permute-done((bf16[128,256]{1,0:T(8,128)(2,1)S(1)}, bf16[128,256]{1,0:T(8,128)(2,1)S(1)}, u32[]{:S(2)}, u32[]{:S(2)}) %collective-permute-start.11) | collective-permute-done | bytes 65568 | tf_op jit(solution)/shard_map/weight_grad/ppermute | solution.py:506
  143.1 3.3 %collective-permute-done.10.refs_2_ = bf16[128,256]{1,0:T(8,128)(2,1)S(1)} collective-permute-done((bf16[128,256]{1,0:T(8,128)(2,1)S(1)}, bf16[128,256]{1,0:T(8,128)(2,1)S(1)}, u32[]{:S(2)}, u32[]{:S(2)}) %collective-permute-start.10) | collective-permute-done | bytes 65568 | tf_op jit(solution)/shard_map/weight_grad/ppermute | solution.py:506
  146.4 0.3 collective-permute-done.9.refs_1_
  146.7 1.6 copy-done.2
  148.3 1.9 %weight_grad.3 = (f32[2,256,256]{2,1,0:T(8,128)S(1)}, bf16[2,256,256]{2,1,0:T(8,128)(2,1)S(1)}) custom-call(s32[2]{0:T(128)S(1)} %pad_add_fusion.at, bf16[128,256]{1,0:T(8,128)(2,1)S(1)} %reduce_sum.24.grad.refs_0_, bf16[128,256]{1,0:T(8,128)(2,1)S(1)} %collective-permute-done.9.refs_1_, bf16[128,256]{1,0:T(8,128)(2,1)S(1)} %collective-permute-done.10.refs_2_, ...), custom_call_target="tpu_custom_call" | custom-call | flops 536870912 | bytes 4194304 | tf_op jit(solution)/shard_map/weight_grad/pallas_call | solution.py:383
  150.2 0.1 collective-permute-start.16
  150.3 0.1 add_convert_fusion
  150.4 1.4 collective-permute-done.16.came
  151.8 1.3 collective-permute-start.17
  153.2 0.7 fusion
  153.9 0.0 all-to-all-done.3
  153.9 2.7 %reduce_sum.25 = bf16[128,1024]{1,0:T(8,128)(2,1)} reduce(bf16[8,128,1024]{2,1,0:T(8,128)(2,1)} %all-to-all-done.3, bf16[]{:T(256)} %constant.48.clone.1), dimensions={0}, to_apply=%region_1.0 | reduce | flops 917504 | bytes 2359298 | tf_op jit(solution)/shard_map/input_grad/reduce_sum | solution.py:502
  156.6 2.4 %collective-permute-done.17.came = bf16[256,256]{1,0:T(8,128)(2,1)S(1)} collective-permute-done((bf16[256,256]{1,0:T(8,128)(2,1)S(1)}, bf16[256,256]{1,0:T(8,128)(2,1)S(1)}, u32[]{:S(2)}, u32[]{:S(2)}) %collective-permute-start.17) | collective-permute-done | bytes 131104 | tf_op jit(solution)/shard_map/weight_grad/ppermute | solution.py:431
  159.0 0.8 weight_grad.5
  (34 shorter events, 0.1 us)
Async XLA Ops:
  7.2 11.1 %copy-start.6 = (bf16[128,512]{1,0:T(8,128)(2,1)S(1)}, bf16[128,512]{1,0:T(8,128)(2,1)}, u32[]{:S(2)}) copy-start(bf16[128,512]{1,0:T(8,128)(2,1)} %param.11) | copy-start | bytes 393220
  7.2 11.1 %copy-start.7 = (bf16[128,512]{1,0:T(8,128)(2,1)S(1)}, bf16[128,512]{1,0:T(8,128)(2,1)}, u32[]{:S(2)}) copy-start(bf16[128,512]{1,0:T(8,128)(2,1)} %param.12) | copy-start | bytes 393220
  7.2 11.1 %copy-start.8 = (bf16[128,512]{1,0:T(8,128)(2,1)S(1)}, bf16[128,512]{1,0:T(8,128)(2,1)}, u32[]{:S(2)}) copy-start(bf16[128,512]{1,0:T(8,128)(2,1)} %param.13) | copy-start | bytes 393220
  8.9 28.8 %all-to-all-start = ((bf16[8,128,256]{2,1,0:T(8,128)(2,1)}), bf16[8,128,256]{2,1,0:T(8,128)(2,1)S(1)}, u32[]{:S(2)}, u32[]{:S(2)}) async-start(bf16[8,128,256]{2,1,0:T(8,128)(2,1)} %broadcast_in_dim.2), calls=%async_computation | async-start | bytes 1048576 | tf_op jit(solution)/shard_map/gather_keys/all_to_all | solution.py:464
  18.3 27.1 %copy-start.9 = (bf16[128,2048]{1,0:T(8,128)(2,1)}, bf16[128,2048]{1,0:T(8,128)(2,1)S(1)}, u32[]{:S(2)}) copy-start(bf16[128,2048]{1,0:T(8,128)(2,1)S(1)} %constant_dynamic-update-slice_fusion.own) | copy-start | bytes 1572868
  18.3 15.0 %collective-permute-start = (bf16[128,2048]{1,0:T(8,128)(2,1)S(1)}, bf16[128,2048]{1,0:T(8,128)(2,1)S(1)}, u32[]{:S(2)}, u32[]{:S(2)}) collective-permute-start(bf16[128,2048]{1,0:T(8,128)(2,1)S(1)} %constant_dynamic-update-slice_fusion.own), channel_id=1, source_target_pairs={{0,128},{128,0},{1,129},{129,1},{2,130},{130,2},{3,131},{131,3},{4... | collective-permute-start | bytes 1572872 | tf_op jit(solution)/shard_map/gather_queries/ppermute | solution.py:431
  21.5 23.9 %collective-permute-start.1 = (bf16[128,2048]{1,0:T(8,128)(2,1)S(1)}, bf16[128,2048]{1,0:T(8,128)(2,1)S(1)}, u32[]{:S(2)}, u32[]{:S(2)}) collective-permute-start(bf16[128,2048]{1,0:T(8,128)(2,1)S(1)} %constant_dynamic-update-slice_fusion.own), channel_id=1, source_target_pairs={{0,8},{8,0},{1,9},{9,1},{2,10},{10,2},{3,11},{11,3},{4,12},{12,4},... | collective-permute-start | bytes 1572872 | tf_op jit(solution)/shard_map/gather_queries/ppermute | solution.py:431
  33.3 12.1 %copy-start.10 = (bf16[128,2048]{1,0:T(8,128)(2,1)}, bf16[128,2048]{1,0:T(8,128)(2,1)S(1)}, u32[]{:S(2)}) copy-start(bf16[128,2048]{1,0:T(8,128)(2,1)S(1)} %collective-permute-done.far) | copy-start | bytes 1572868
  33.3 12.1 %collective-permute-start.2 = (bf16[128,2048]{1,0:T(8,128)(2,1)S(1)}, bf16[128,2048]{1,0:T(8,128)(2,1)S(1)}, u32[]{:S(2)}, u32[]{:S(2)}) collective-permute-start(bf16[128,2048]{1,0:T(8,128)(2,1)S(1)} %collective-permute-done.far), channel_id=1, source_target_pairs={{0,8},{8,0},{1,9},{9,1},{2,10},{10,2},{3,11},{11,3},{4,12},{12,4},... | collective-permute-start | bytes 1572872 | tf_op jit(solution)/shard_map/gather_queries/ppermute | solution.py:431
  37.7 7.7 %copy-start.5 = (bf16[8,128,256]{2,1,0:T(8,128)(2,1)}, bf16[8,128,256]{2,1,0:T(8,128)(2,1)S(1)}, u32[]{:S(2)}) copy-start(bf16[8,128,256]{2,1,0:T(8,128)(2,1)S(1)} %all-to-all-done.kv) | copy-start | bytes 1572868
  37.7 24.3 %all-to-all-start.1 = ((bf16[8,128,128]{2,1,0:T(8,128)(2,1)}), bf16[8,128,128]{2,1,0:T(8,128)(2,1)S(1)}, u32[]{:S(2)}, u32[]{:S(2)}) async-start(bf16[8,128,128]{2,1,0:T(8,128)(2,1)} %cut_input.1), calls=%async_computation.1 | async-start | bytes 524288 | tf_op jit(solution)/shard_map/spread_input/all_to_all | solution.py:482
  44.6 102.1 %all-gather.2.cloned.1.call-start = ((), (), s32[]{:S(2)}) async-start(), calls=%async_computation.4 | async-start | bytes 2359296 | tf_op jit(solution)/shard_map/spread_input/all_gather | solution.py:489
  45.4 0.8 copy-start.11
  46.2 0.8 copy-start.12
  58.2 5.7 %collective-permute-start.5 = (f32[3,8,512]{2,1,0:T(8,128)}, f32[3,8,512]{2,1,0:T(8,128)S(1)}, u32[]{:S(2)}, u32[]{:S(2)}) collective-permute-start(f32[3,8,512]{2,1,0:T(8,128)} %attention_stats.1.s_own), channel_id=1, source_target_pairs={{0,136},{8,128},{128,8},{136,0},{1,137},{9,129},{129,9},{137,1},{2... | collective-permute-start | bytes 147464 | tf_op jit(solution)/shard_map/share_stats/ppermute | solution.py:435
  60.2 3.8 %collective-permute-start.4 = (f32[3,8,512]{2,1,0:T(8,128)}, f32[3,8,512]{2,1,0:T(8,128)S(1)}, u32[]{:S(2)}, u32[]{:S(2)}) collective-permute-start(f32[3,8,512]{2,1,0:T(8,128)} %attention_stats.1.s_own), channel_id=1, source_target_pairs={{0,8},{8,0},{1,9},{9,1},{2,10},{10,2},{3,11},{11,3},{4,12},{12,4},... | collective-permute-start | bytes 147464 | tf_op jit(solution)/shard_map/share_stats/ppermute | solution.py:431
  60.2 5.9 %collective-permute-start.3 = (f32[3,8,512]{2,1,0:T(8,128)}, f32[3,8,512]{2,1,0:T(8,128)S(1)}, u32[]{:S(2)}, u32[]{:S(2)}) collective-permute-start(f32[3,8,512]{2,1,0:T(8,128)} %attention_stats.1.s_own), channel_id=1, source_target_pairs={{0,128},{128,0},{1,129},{129,1},{2,130},{130,2},{3,131},{131,3},{4... | collective-permute-start | bytes 147464 | tf_op jit(solution)/shard_map/share_stats/ppermute | solution.py:431
  62.0 4.1 %copy-start.3 = (bf16[8,128,128]{2,1,0:T(8,128)(2,1)}, bf16[8,128,128]{2,1,0:T(8,128)(2,1)S(1)}, u32[]{:S(2)}) copy-start(bf16[8,128,128]{2,1,0:T(8,128)(2,1)S(1)} %all-to-all-done.1) | copy-start | bytes 786436
  64.0 2.1 %copy-start.13 = (f32[3,8,512]{2,1,0:T(8,128)}, f32[3,8,512]{2,1,0:T(8,128)S(1)}, u32[]{:S(2)}) copy-start(f32[3,8,512]{2,1,0:T(8,128)S(1)} %collective-permute-done.5.s_both) | copy-start | bytes 147460
  64.0 2.1 %copy-start.14 = (f32[3,8,512]{2,1,0:T(8,128)}, f32[3,8,512]{2,1,0:T(8,128)S(1)}, u32[]{:S(2)}) copy-start(f32[3,8,512]{2,1,0:T(8,128)S(1)} %collective-permute-done.4.s_side) | copy-start | bytes 147460
  66.1 0.6 copy-start.15
  66.7 46.6 %copy-start = (bf16[8192,128]{1,0:T(8,128)(2,1)S(1)}, bf16[8192,128]{1,0:T(8,128)(2,1)}, u32[]{:S(2)}) copy-start(bf16[8192,128]{1,0:T(8,128)(2,1)} %key_weight.1) | copy-start | bytes 6291460
  80.6 32.7 %all-to-all-start.2 = ((bf16[8,128,256]{2,1,0:T(8,128)(2,1)}), bf16[8,128,256]{2,1,0:T(8,128)(2,1)S(1)}, u32[]{:S(2)}, u32[]{:S(2)}) async-start(bf16[8,128,256]{2,1,0:T(8,128)(2,1)} %get-tuple-element.36), calls=%async_computation.2 | async-start | bytes 1048576 | tf_op jit(solution)/shard_map/scatter_grads/all_to_all | solution.py:492
  87.9 16.5 %collective-permute-start.6 = (bf16[128,1024]{1,0:T(8,128)(2,1)}, bf16[128,1024]{1,0:T(8,128)(2,1)S(1)}, u32[]{:S(2)}, u32[]{:S(2)}) collective-permute-start(bf16[128,1024]{1,0:T(8,128)(2,1)} %get-tuple-element.37), channel_id=1, source_target_pairs={{0,128},{128,0},{1,129},{129,1},{2,130},{130,2},{3,131},{131,3},{4... | collective-permute-start | bytes 786440 | tf_op jit(solution)/shard_map/scatter_grads/ppermute | solution.py:431
  89.8 14.6 %collective-permute-start.7 = (bf16[128,1024]{1,0:T(8,128)(2,1)}, bf16[128,1024]{1,0:T(8,128)(2,1)S(1)}, u32[]{:S(2)}, u32[]{:S(2)}) collective-permute-start(bf16[128,1024]{1,0:T(8,128)(2,1)} %get-tuple-element.38), channel_id=1, source_target_pairs={{0,8},{8,0},{1,9},{9,1},{2,10},{10,2},{3,11},{11,3},{4,12},{12,4},... | collective-permute-start | bytes 786440 | tf_op jit(solution)/shard_map/scatter_grads/ppermute | solution.py:431
  89.8 23.4 %collective-permute-start.8 = (bf16[128,1024]{1,0:T(8,128)(2,1)}, bf16[128,1024]{1,0:T(8,128)(2,1)S(1)}, u32[]{:S(2)}, u32[]{:S(2)}) collective-permute-start(bf16[128,1024]{1,0:T(8,128)(2,1)} %get-tuple-element.39), channel_id=1, source_target_pairs={{0,136},{8,128},{128,8},{136,0},{1,137},{9,129},{129,9},{137,1},{2... | collective-permute-start | bytes 786440 | tf_op jit(solution)/shard_map/scatter_grads/ppermute | solution.py:435
  113.3 1.6 copy-start.1
  117.6 32.7 %copy-start.4 = (f32[128,1024]{1,0:T(8,128)S(1)}, f32[128,1024]{1,0:T(8,128)}, u32[]{:S(2)}) copy-start(f32[128,1024]{1,0:T(8,128)} %get-tuple-element.35) | copy-start | bytes 1572868
  117.6 36.3 %all-to-all-start.3 = ((bf16[8,128,1024]{2,1,0:T(8,128)(2,1)}), bf16[8,128,1024]{2,1,0:T(8,128)(2,1)}, u32[]{:S(2)}, u32[]{:S(2)}) async-start(bf16[8,128,1024]{2,1,0:T(8,128)(2,1)} %input_grad.1), calls=%async_computation.3 | async-start | bytes 4194304 | tf_op jit(solution)/shard_map/input_grad/all_to_all | solution.py:501
  122.3 10.6 %collective-permute-start.15 = (bf16[128,256]{1,0:T(8,128)(2,1)S(1)}, bf16[128,256]{1,0:T(8,128)(2,1)S(1)}, u32[]{:S(2)}, u32[]{:S(2)}) collective-permute-start(bf16[128,256]{1,0:T(8,128)(2,1)S(1)} %reduce_sum.24.grad.refs_0_), channel_id=1, source_target_pairs={{0,112},{16,0},{32,16},{48,32},{64,48},{80,64},{96,80},{112,96},{1... | collective-permute-start | bytes 196616 | tf_op jit(solution)/shard_map/weight_grad/ppermute | solution.py:506
  125.4 11.0 %collective-permute-start.14 = (bf16[128,256]{1,0:T(8,128)(2,1)S(1)}, bf16[128,256]{1,0:T(8,128)(2,1)S(1)}, u32[]{:S(2)}, u32[]{:S(2)}) collective-permute-start(bf16[128,256]{1,0:T(8,128)(2,1)S(1)} %reduce_sum.24.grad.refs_0_), channel_id=1, source_target_pairs={{0,96},{16,112},{32,0},{48,16},{64,32},{80,48},{96,64},{112,80},{1... | collective-permute-start | bytes 196616 | tf_op jit(solution)/shard_map/weight_grad/ppermute | solution.py:506
  127.8 10.3 %collective-permute-start.13 = (bf16[128,256]{1,0:T(8,128)(2,1)S(1)}, bf16[128,256]{1,0:T(8,128)(2,1)S(1)}, u32[]{:S(2)}, u32[]{:S(2)}) collective-permute-start(bf16[128,256]{1,0:T(8,128)(2,1)S(1)} %reduce_sum.24.grad.refs_0_), channel_id=1, source_target_pairs={{0,80},{16,96},{32,112},{48,0},{64,16},{80,32},{96,48},{112,64},{1... | collective-permute-start | bytes 196616 | tf_op jit(solution)/shard_map/weight_grad/ppermute | solution.py:506
  128.9 10.0 %collective-permute-start.12 = (bf16[128,256]{1,0:T(8,128)(2,1)S(1)}, bf16[128,256]{1,0:T(8,128)(2,1)S(1)}, u32[]{:S(2)}, u32[]{:S(2)}) collective-permute-start(bf16[128,256]{1,0:T(8,128)(2,1)S(1)} %reduce_sum.24.grad.refs_0_), channel_id=1, source_target_pairs={{0,64},{16,80},{32,96},{48,112},{64,0},{80,16},{96,32},{112,48},{1... | collective-permute-start | bytes 196616 | tf_op jit(solution)/shard_map/weight_grad/ppermute | solution.py:506
  132.9 10.2 %collective-permute-start.11 = (bf16[128,256]{1,0:T(8,128)(2,1)S(1)}, bf16[128,256]{1,0:T(8,128)(2,1)S(1)}, u32[]{:S(2)}, u32[]{:S(2)}) collective-permute-start(bf16[128,256]{1,0:T(8,128)(2,1)S(1)} %reduce_sum.24.grad.refs_0_), channel_id=1, source_target_pairs={{0,48},{16,64},{32,80},{48,96},{64,112},{80,0},{96,16},{112,32},{1... | collective-permute-start | bytes 196616 | tf_op jit(solution)/shard_map/weight_grad/ppermute | solution.py:506
  132.9 13.5 %collective-permute-start.10 = (bf16[128,256]{1,0:T(8,128)(2,1)S(1)}, bf16[128,256]{1,0:T(8,128)(2,1)S(1)}, u32[]{:S(2)}, u32[]{:S(2)}) collective-permute-start(bf16[128,256]{1,0:T(8,128)(2,1)S(1)} %reduce_sum.24.grad.refs_0_), channel_id=1, source_target_pairs={{0,32},{16,48},{32,64},{48,80},{64,96},{80,112},{96,0},{112,16},{1... | collective-permute-start | bytes 196616 | tf_op jit(solution)/shard_map/weight_grad/ppermute | solution.py:506
  136.4 10.3 %collective-permute-start.9 = (bf16[128,256]{1,0:T(8,128)(2,1)S(1)}, bf16[128,256]{1,0:T(8,128)(2,1)S(1)}, u32[]{:S(2)}, u32[]{:S(2)}) collective-permute-start(bf16[128,256]{1,0:T(8,128)(2,1)S(1)} %reduce_sum.24.grad.refs_0_), channel_id=1, source_target_pairs={{0,16},{16,32},{32,48},{48,64},{64,80},{80,96},{96,112},{112,0},{1... | collective-permute-start | bytes 196616 | tf_op jit(solution)/shard_map/weight_grad/ppermute | solution.py:506
  146.7 1.6 copy-start.2
  150.2 1.6 collective-permute-start.16
  151.8 7.1 %collective-permute-start.17 = (bf16[256,256]{1,0:T(8,128)(2,1)S(1)}, bf16[256,256]{1,0:T(8,128)(2,1)S(1)}, u32[]{:S(2)}, u32[]{:S(2)}) collective-permute-start(bf16[256,256]{1,0:T(8,128)(2,1)S(1)} %get-tuple-element.48), channel_id=1, source_target_pairs={{0,128},{128,0},{1,129},{129,1},{2,130},{130,2},{3,131},{131,3},{4... | collective-permute-start | bytes 393224 | tf_op jit(solution)/shard_map/weight_grad/ppermute | solution.py:431
Sparse Core Ops, SparseCore 0:
  66.2 47.3 all-gather.1
